TPU v7x, 512 devices: a whole 4x8x8 slice. The times are simulated.
512 devices in a mesh: seq: 64 (over x, y_hi, z), chan: 8 (over y_lo, core).
Axes of the slice: x: 4, y: 8 (y_hi: 2, y_lo: 4; y = y_hi * 4 + y_lo), z: 8, core: 2. Of those that a mesh axis runs over, the one named last changes fastest.
Arguments:
- inputs: bfloat16 [3, 256, 16384], P(None, 'chan', 'seq'), may hold values from -6 to 6
- short_weights: float32 [3, 3, 256], P(None, None, 'chan'), may hold values from -3 to 3
- filters: float32 [32, 16384], P(None, 'seq'), may hold values from -1.2 to 1.2
- skip: float32 [256], P('chan'), may hold values from -4 to 4
- grad_out: bfloat16 [256, 16384], P('chan', 'seq'), may hold values from -7.5 to 7.5
Outputs:
- input_grads: float32 [3, 256, 16384], P(None, 'chan', 'seq')
- filter_grad: float32 [32, 16384], P('chan', 'seq')
- skip_grad: float32 [256], P('chan')
- short_grad: float32 [3, 3, 256], P(None, None, 'chan')
All inputs are finite; a program needn't handle non-finite values.
Results may differ from a plain program's by a relative error of at most 0.0003.
Values may be sent and summed in bfloat16 or wider, within the bound.
No kernel may reach another device: no remote copies, remote signals or barrier semaphores. Data moves between devices by JAX's collectives and lax.ppermute only.
A program may use at most 64 MiB of HBM per device.

v0:
```python
import math

import jax
import jax.numpy as jnp
from jax import lax
from jax.sharding import PartitionSpec as P

highest = lax.Precision.HIGHEST


def shifted(block, axis, distance):
    devices = range(lax.axis_size(axis))
    route = [(i - distance, i) for i in devices if i - distance in devices]
    return lax.ppermute(block, axis, route)


def angle_table(rows, cols, period, sign):
    grid = (
        jnp.arange(rows, dtype=jnp.int32)[:, None]
        * jnp.arange(cols, dtype=jnp.int32)[None, :]
        % period
    )
    angle = sign * 2.0 * math.pi / period * grid.astype(jnp.float32)
    return (jnp.cos(angle), jnp.sin(angle))


def rotate(real_part, imag_part, cosine, sine):
    return (real_part * cosine - imag_part * sine, real_part * sine + imag_part * cosine)


def transform_last(real_part, imag_part, sign):
    length = real_part.shape[-1]
    if length <= 128 or length % 64 != 0:
        cosine, sine = angle_table(length, length, length, sign)
        new_real = jnp.dot(real_part, cosine, precision=highest) - jnp.dot(
            imag_part, sine, precision=highest
        )
        new_imag = jnp.dot(real_part, sine, precision=highest) + jnp.dot(
            imag_part, cosine, precision=highest
        )
        return (new_real, new_imag)
    outer = 64
    inner = length // outer
    leading = real_part.shape[:-1]
    real_part = jnp.swapaxes(real_part.reshape(leading + (inner, outer)), -1, -2)
    imag_part = jnp.swapaxes(imag_part.reshape(leading + (inner, outer)), -1, -2)
    real_part, imag_part = transform_last(real_part, imag_part, sign)
    cosine, sine = angle_table(outer, inner, length, sign)
    real_part, imag_part = rotate(real_part, imag_part, cosine, sine)
    cosine, sine = angle_table(outer, outer, outer, sign)
    new_real = jnp.einsum("...jk,jl->...lk", real_part, cosine, precision=highest) - jnp.einsum(
        "...jk,jl->...lk", imag_part, sine, precision=highest
    )
    new_imag = jnp.einsum("...jk,jl->...lk", real_part, sine, precision=highest) + jnp.einsum(
        "...jk,jl->...lk", imag_part, cosine, precision=highest
    )
    return (new_real.reshape(leading + (length,)), new_imag.reshape(leading + (length,)))


def forward_spectrum(stacked):
    parts = lax.axis_size("seq")
    rank = lax.axis_index("seq")
    span = stacked.shape[2]
    width = span // parts
    period = 2 * span * parts
    rows = lax.all_to_all(stacked[:, :, None, :], "seq", split_axis=3, concat_axis=2, tiled=True)
    cosine, sine = angle_table(parts, 2 * parts, 2 * parts, -1.0)
    real_part = jnp.einsum("bcpm,pq->bcqm", rows, cosine, precision=highest)
    imag_part = jnp.einsum("bcpm,pq->bcqm", rows, sine, precision=highest)
    column = rank * width + jnp.arange(width, dtype=jnp.int32)
    grid = jnp.arange(2 * parts, dtype=jnp.int32)[:, None] * column[None, :] % period
    angle = -2.0 * math.pi / period * grid.astype(jnp.float32)
    real_part, imag_part = rotate(real_part, imag_part, jnp.cos(angle), jnp.sin(angle))
    real_part, imag_part = (
        lax.all_to_all(real_part, "seq", split_axis=2, concat_axis=3, tiled=True),
        lax.all_to_all(imag_part, "seq", split_axis=2, concat_axis=3, tiled=True),
    )
    return transform_last(real_part, imag_part, -1.0)


def inverse_start(real_part, imag_part):
    parts = lax.axis_size("seq")
    rank = lax.axis_index("seq")
    span = real_part.shape[3]
    period = 2 * span * parts
    real_part, imag_part = transform_last(real_part, imag_part, 1.0)
    residue = 2 * rank + jnp.arange(2, dtype=jnp.int32)
    grid = residue[:, None] * jnp.arange(span, dtype=jnp.int32)[None, :] % period
    angle = 2.0 * math.pi / period * grid.astype(jnp.float32)
    return rotate(real_part, imag_part, jnp.cos(angle), jnp.sin(angle))


def inverse_finish(real_part, imag_part, period):
    parts = lax.axis_size("seq")
    cosine, sine = angle_table(2 * parts, parts, 2 * parts, 1.0)
    new_real = jnp.einsum("bcqm,qp->bcpm", real_part, cosine, precision=highest) - jnp.einsum(
        "bcqm,qp->bcpm", imag_part, sine, precision=highest
    )
    new_imag = jnp.einsum("bcqm,qp->bcpm", real_part, sine, precision=highest) + jnp.einsum(
        "bcqm,qp->bcpm", imag_part, cosine, precision=highest
    )
    return (new_real * (1.0 / period), new_imag * (1.0 / period))


def body(inputs, short_weights, filters, skip, grad_out):
    taps = short_weights.shape[1]
    parts = lax.axis_size("seq")
    groups = lax.axis_size("chan")
    span = inputs.shape[2]
    channels = inputs.shape[1]
    total = span * parts
    period = 2 * total
    border = shifted(inputs[:, :, span - (taps - 1) :], "seq", 1)
    extended = jnp.concatenate([border, inputs], axis=2).astype(jnp.float32)
    mixed = short_weights[:, 0, :, None] * extended[:, :, taps - 1 : taps - 1 + span]
    for offset in range(1, taps):
        start = taps - 1 - offset
        mixed = mixed + short_weights[:, offset, :, None] * extended[:, :, start : start + span]
    query, key_part, value = (mixed[0], mixed[1], mixed[2])
    grad = grad_out.astype(jnp.float32)
    product = key_part * value
    dw = grad * query
    spec_real, spec_imag = forward_spectrum(jnp.stack([product, dw, filters]))
    prod_real, grad_real, filt_real = (spec_real[0], spec_real[1], spec_real[2])
    prod_imag, grad_imag, filt_imag = (spec_imag[0], spec_imag[1], spec_imag[2])
    conv_real = filt_real * prod_real - filt_imag * prod_imag
    conv_imag = filt_real * prod_imag + filt_imag * prod_real
    back_real = grad_real * filt_real + grad_imag * filt_imag
    back_imag = grad_imag * filt_real - grad_real * filt_imag
    corr_real = grad_real * prod_real + grad_imag * prod_imag
    corr_imag = grad_imag * prod_real - grad_real * prod_imag
    start_real, start_imag = inverse_start(
        jnp.stack([conv_real, back_real, corr_real]), jnp.stack([conv_imag, back_imag, corr_imag])
    )
    start_real, start_imag = (
        lax.all_to_all(start_real, "seq", split_axis=3, concat_axis=2, tiled=True),
        lax.all_to_all(start_imag, "seq", split_axis=3, concat_axis=2, tiled=True),
    )
    result, unused = inverse_finish(start_real, start_imag, period)
    fields = lax.all_to_all(result, "seq", split_axis=2, concat_axis=3, tiled=True).reshape(
        3, channels, span
    )
    conv_out = fields[0] + skip[:, None] * product
    dz = fields[1] + skip[:, None] * dw
    filter_grad = lax.psum_scatter(
        fields[2] * (total * groups) ** (-0.5), "chan", scatter_dimension=0, tiled=True
    )
    grads = jnp.stack([grad * conv_out, dz * value, dz * key_part])
    after = shifted(grads[:, :, : taps - 1], "seq", -1)
    grad_ext = jnp.concatenate([grads, after], axis=2)
    in_grads = short_weights[:, 0, :, None] * grads
    for offset in range(1, taps):
        in_grads = (
            in_grads + short_weights[:, offset, :, None] * grad_ext[:, :, offset : offset + span]
        )
    short_rows = []
    for offset in range(taps):
        start = taps - 1 - offset
        short_rows.append(jnp.sum(grads * extended[:, :, start : start + span], axis=2))
    short_part = jnp.stack(short_rows, axis=1)
    skip_part = jnp.sum(dw * product, axis=1)
    short_sum, skip_sum = lax.psum((short_part, skip_part), "seq")
    scale = total ** (-0.5)
    return (in_grads, filter_grad, skip_sum * scale, short_sum * scale)


def solution(mesh):
    placed = (
        P(None, "chan", "seq"),
        P(None, None, "chan"),
        P(None, "seq"),
        P("chan"),
        P("chan", "seq"),
    )
    return jax.shard_map(
        body,
        mesh=mesh,
        in_specs=placed,
        out_specs=(P(None, "chan", "seq"), P("chan", "seq"), P("chan"), P(None, None, "chan")),
        check_vma=False,
    )
```

profile of v0, /device:TPU:64, one launch (start us, length us, event | category | flops | bytes accessed | tf_op | source)
XLA Modules:
  0.0 425.2 jit_solution(2603154138270515414)
XLA Ops:
  0.6 0.8 slice.83
  1.5 4.3 %collective-permute-start = (bf16[3,32,2]{2,1,0:T(8,128)(2,1)S(1)}, bf16[3,32,2]{2,1,0:T(8,128)(2,1)S(1)}, u32[]{:S(2)}, u32[]{:S(2)}) collective-permute-start(bf16[3,32,2]{2,1,0:T(8,128)(2,1)S(1)} %slice.83), channel_id=1, source_target_pairs={{0,8},{8,16},{16,24},{24,32},{32,40},{40,48},{48,56},{56,64},{64,7... | collective-permute-start | bytes 1160 | tf_op jit(solution)/shard_map/ppermute | solution.py:14
  6.7 2.9 collective-permute-done
  10.2 0.7 copy-done.3
  11.8 2.0 reduce
  13.8 1.0 reshape.518
  14.7 17.0 %all-to-all-start = ((f32[64,1,384]{2,1,0:T(1,128)}), f32[64,1,384]{2,1,0:T(1,128)S(1)}, u32[]{:S(2)}, u32[]{:S(2)}) async-start(f32[64,1,384]{2,1,0:T(1,128)} %reshape.518), calls=%async_computation | async-start | bytes 196608 | tf_op jit(solution)/shard_map/all_to_all | solution.py:66
  31.9 13.4 %all-to-all-done = f32[64,1,384]{2,1,0:T(1,128)S(1)} async-done(((f32[64,1,384]{2,1,0:T(1,128)}), f32[64,1,384]{2,1,0:T(1,128)S(1)}, u32[]{:S(2)}, u32[]{:S(2)}) %all-to-all-start) | async-done | bytes 98336 | tf_op jit(solution)/shard_map/all_to_all | solution.py:66
  45.3 0.9 reduce.1
  46.2 0.7 reshape.519
  48.4 1.2 reshape.520
  49.6 5.5 %all-to-all-start.1 = ((f32[64,1,768]{2,1,0:T(1,128)}), f32[64,1,768]{2,1,0:T(1,128)S(1)}, u32[]{:S(2)}, u32[]{:S(2)}) async-start(f32[64,1,768]{2,1,0:T(1,128)} %reshape.520), calls=%async_computation.1 | async-start | bytes 393216 | tf_op jit(solution)/shard_map/all_to_all | solution.py:75
  55.1 0.7 fusion.106
  56.2 1.2 reshape.522
  57.4 11.8 %all-to-all-done.1 = f32[64,1,768]{2,1,0:T(1,128)S(1)} async-done(((f32[64,1,768]{2,1,0:T(1,128)}), f32[64,1,768]{2,1,0:T(1,128)S(1)}, u32[]{:S(2)}, u32[]{:S(2)}) %all-to-all-start.1) | async-done | bytes 196640 | tf_op jit(solution)/shard_map/all_to_all | solution.py:75
  69.2 6.1 %all-to-all-start.2 = ((f32[64,1,768]{2,1,0:T(1,128)}), f32[64,1,768]{2,1,0:T(1,128)S(1)}, u32[]{:S(2)}, u32[]{:S(2)}) async-start(f32[64,1,768]{2,1,0:T(1,128)} %reshape.522), calls=%async_computation.2 | async-start | bytes 393216 | tf_op jit(solution)/shard_map/all_to_all | solution.py:76
  75.3 1.1 reduce.2
  77.7 0.8 fusion.12
  78.5 0.8 fusion.10
  79.3 9.8 %all-to-all-done.2 = f32[64,1,768]{2,1,0:T(1,128)S(1)} async-done(((f32[64,1,768]{2,1,0:T(1,128)}), f32[64,1,768]{2,1,0:T(1,128)S(1)}, u32[]{:S(2)}, u32[]{:S(2)}) %all-to-all-start.2) | async-done | bytes 196640 | tf_op jit(solution)/shard_map/all_to_all | solution.py:76
  89.2 1.1 reduce.3
  91.6 0.9 convolution_subtract_fusion.3
  92.4 1.0 multiply_add_fusion.2
  96.9 0.9 fusion.26
  97.7 0.9 fusion.27
  99.7 0.9 convolution_subtract_fusion.1
  100.6 1.0 multiply_add_fusion.1
  106.3 1.5 reshape.524
  107.8 5.8 %all-to-all-start.3 = ((f32[64,1,768]{2,1,0:T(1,128)}), f32[64,1,768]{2,1,0:T(1,128)S(1)}, u32[]{:S(2)}, u32[]{:S(2)}) async-start(f32[64,1,768]{2,1,0:T(1,128)} %reshape.524), calls=%async_computation.3 | async-start | bytes 393216 | tf_op jit(solution)/shard_map/all_to_all | solution.py:136
  114.3 1.5 reshape.526
  115.8 11.9 %all-to-all-done.3 = f32[64,1,768]{2,1,0:T(1,128)S(1)} async-done(((f32[64,1,768]{2,1,0:T(1,128)}), f32[64,1,768]{2,1,0:T(1,128)S(1)}, u32[]{:S(2)}, u32[]{:S(2)}) %all-to-all-start.3) | async-done | bytes 196640 | tf_op jit(solution)/shard_map/all_to_all | solution.py:136
  127.7 6.2 %all-to-all-start.4 = ((f32[64,1,768]{2,1,0:T(1,128)}), f32[64,1,768]{2,1,0:T(1,128)S(1)}, u32[]{:S(2)}, u32[]{:S(2)}) async-start(f32[64,1,768]{2,1,0:T(1,128)} %reshape.526), calls=%async_computation.4 | async-start | bytes 393216 | tf_op jit(solution)/shard_map/all_to_all | solution.py:137
  133.9 1.1 reduce.4
  136.4 1.4 fusion.44
  137.8 10.1 %all-to-all-done.4 = f32[64,1,768]{2,1,0:T(1,128)S(1)} async-done(((f32[64,1,768]{2,1,0:T(1,128)}), f32[64,1,768]{2,1,0:T(1,128)S(1)}, u32[]{:S(2)}, u32[]{:S(2)}) %all-to-all-start.4) | async-done | bytes 196640 | tf_op jit(solution)/shard_map/all_to_all | solution.py:137
  147.8 1.1 reduce.5
  150.3 1.4 fusion.5
  151.9 0.9 reshape.528
  152.8 5.8 %all-to-all-start.5 = ((f32[64,1,384]{2,1,0:T(1,128)}), f32[64,1,384]{2,1,0:T(1,128)S(1)}, u32[]{:S(2)}, u32[]{:S(2)}) async-start(f32[64,1,384]{2,1,0:T(1,128)} %reshape.528), calls=%async_computation.5 | async-start | bytes 196608 | tf_op jit(solution)/shard_map/all_to_all | solution.py:140
  158.6 1.3 dynamic-slice
  160.6 11.6 %all-to-all-done.5 = f32[64,1,384]{2,1,0:T(1,128)S(1)} async-done(((f32[64,1,384]{2,1,0:T(1,128)}), f32[64,1,384]{2,1,0:T(1,128)S(1)}, u32[]{:S(2)}, u32[]{:S(2)}) %all-to-all-start.5) | async-done | bytes 98336 | tf_op jit(solution)/shard_map/all_to_all | solution.py:140
  172.2 0.9 reduce.6
  173.4 0.7 copy-done.1
  174.3 3.3 collective-permute-start.1
  177.6 27.2 %all-reduce = f32[32,256]{0,1:T(8,128)S(1)} all-reduce(f32[32,256]{0,1:T(8,128)S(1)} %bitcast.251), channel_id=2, replica_groups=mesh['seq'=64,'chan'=8] {'chan'}, use_global_device_ids=true, to_apply=%region_0.1.clone | all-reduce | flops 8192 | bytes 65536
  204.9 0.7 copy.343
  206.6 216.3 %all-reduce.1 = (f32[32]{0:T(128)S(1)}, f32[3,3,32]{2,0,1:T(4,128)S(1)}) all-reduce(f32[32]{0:T(128)S(1)} %get-tuple-element.52, f32[3,3,32]{2,0,1:T(4,128)S(1)} %pad_maximum_fusion.3), channel_id=1, replica_groups=mesh['seq'=64,'chan'=8] {'seq'}, use_global_device_ids=true, to_apply=%region_2.3 | all-reduce | flops 320 | bytes 2560 | tf_op jit(solution)/shard_map/psum | solution.py:162
  424.0 0.8 copy.342
  (105 shorter events, 21.9 us)
Async XLA Ops:
  0.6 5.2 %copy-start.11 = (f32[3,3,32]{2,1,0:T(4,128)S(1)}, f32[3,3,32]{2,1,0:T(4,128)}, u32[]{:S(2)}) copy-start(f32[3,3,32]{2,1,0:T(4,128)} %param.6) | copy-start | bytes 3460
  1.5 8.1 %collective-permute-start = (bf16[3,32,2]{2,1,0:T(8,128)(2,1)S(1)}, bf16[3,32,2]{2,1,0:T(8,128)(2,1)S(1)}, u32[]{:S(2)}, u32[]{:S(2)}) collective-permute-start(bf16[3,32,2]{2,1,0:T(8,128)(2,1)S(1)} %slice.83), channel_id=1, source_target_pairs={{0,8},{8,16},{16,24},{24,32},{32,40},{40,48},{48,56},{56,64},{64,7... | collective-permute-start | bytes 1160 | tf_op jit(solution)/shard_map/ppermute | solution.py:14
  5.8 0.7 copy-start.8
  5.8 3.7 copy-start.2
  5.9 4.0 copy-start.4
  6.5 3.4 copy-start.6
  6.6 3.4 copy-start
  10.1 0.8 copy-start.3
  14.7 30.6 %all-to-all-start = ((f32[64,1,384]{2,1,0:T(1,128)}), f32[64,1,384]{2,1,0:T(1,128)S(1)}, u32[]{:S(2)}, u32[]{:S(2)}) async-start(f32[64,1,384]{2,1,0:T(1,128)} %reshape.518), calls=%async_computation | async-start | bytes 196608 | tf_op jit(solution)/shard_map/all_to_all | solution.py:66
  49.6 19.6 %all-to-all-start.1 = ((f32[64,1,768]{2,1,0:T(1,128)}), f32[64,1,768]{2,1,0:T(1,128)S(1)}, u32[]{:S(2)}, u32[]{:S(2)}) async-start(f32[64,1,768]{2,1,0:T(1,128)} %reshape.520), calls=%async_computation.1 | async-start | bytes 393216 | tf_op jit(solution)/shard_map/all_to_all | solution.py:75
  69.2 19.9 %all-to-all-start.2 = ((f32[64,1,768]{2,1,0:T(1,128)}), f32[64,1,768]{2,1,0:T(1,128)S(1)}, u32[]{:S(2)}, u32[]{:S(2)}) async-start(f32[64,1,768]{2,1,0:T(1,128)} %reshape.522), calls=%async_computation.2 | async-start | bytes 393216 | tf_op jit(solution)/shard_map/all_to_all | solution.py:76
  104.7 0.7 copy-start.10
  104.8 0.7 copy-start.9
  107.8 19.9 %all-to-all-start.3 = ((f32[64,1,768]{2,1,0:T(1,128)}), f32[64,1,768]{2,1,0:T(1,128)S(1)}, u32[]{:S(2)}, u32[]{:S(2)}) async-start(f32[64,1,768]{2,1,0:T(1,128)} %reshape.524), calls=%async_computation.3 | async-start | bytes 393216 | tf_op jit(solution)/shard_map/all_to_all | solution.py:136
  127.7 20.1 %all-to-all-start.4 = ((f32[64,1,768]{2,1,0:T(1,128)}), f32[64,1,768]{2,1,0:T(1,128)S(1)}, u32[]{:S(2)}, u32[]{:S(2)}) async-start(f32[64,1,768]{2,1,0:T(1,128)} %reshape.526), calls=%async_computation.4 | async-start | bytes 393216 | tf_op jit(solution)/shard_map/all_to_all | solution.py:137
  152.8 19.4 %all-to-all-start.5 = ((f32[64,1,384]{2,1,0:T(1,128)}), f32[64,1,384]{2,1,0:T(1,128)S(1)}, u32[]{:S(2)}, u32[]{:S(2)}) async-start(f32[64,1,384]{2,1,0:T(1,128)} %reshape.528), calls=%async_computation.5 | async-start | bytes 196608 | tf_op jit(solution)/shard_map/all_to_all | solution.py:140
  173.3 0.8 copy-start.1
  173.4 0.7 copy-start.12
  174.3 31.3 %collective-permute-start.1 = (f32[3,32,2]{1,2,0:T(2,128)S(1)}, f32[3,32,2]{1,2,0:T(2,128)S(1)}, u32[]{:S(2)}, u32[]{:S(2)}) collective-permute-start(f32[3,32,2]{1,2,0:T(2,128)S(1)} %slice.118), channel_id=1, source_target_pairs={{8,0},{16,8},{24,16},{32,24},{40,32},{48,40},{56,48},{64,56},{72,6... | collective-permute-start | bytes 2312 | tf_op jit(solution)/shard_map/ppermute | solution.py:14
  205.6 0.7 copy-start.5
  205.6 0.7 copy-start.7
where the time goes:
time: 432 us; the launch traced here: 425 us
  blocking collectives  243 us (56%)
  waiting for transfers between devices  71.6 us (17%)
  starting transfers between devices  54 us (12%)
  local copies, waits for them, and re-layouts  27.1 us (6%)
  matrix products  15.6 us (4%)
  other arithmetic  10.9 us (3%)
    psum x1, blocking collectives, body(): short_sum, skip_sum = lax.psum((short_part, skip_part), 'seq')  216 us
    unnamed x1, blocking collectives  27.2 us
    unnamed x47, local copies, waits for them, and re-layouts  17.7 us
    all_to_all x1, starting transfers between devices, forward_spectrum(): lax.all_to_all(stacked[:, :, None, :], 'seq', split_axis=3, concat_axis=2...  17 us
    all_to_all x1, waiting for transfers between devices, forward_spectrum(): lax.all_to_all(stacked[:, :, None, :], 'seq', split_axis=3, concat_axis=2...  13.4 us
    all_to_all x1, waiting for transfers between devices, body(): lax.all_to_all(start_real, 'seq', split_axis=3, concat_axis=2, tiled=True)  11.9 us
    all_to_all x1, waiting for transfers between devices, forward_spectrum(): lax.all_to_all(real_part, 'seq', split_axis=2, concat_axis=3, tiled=True)  11.8 us
    all_to_all x1, waiting for transfers between devices, body(): lax.all_to_all(result, 'seq', split_axis=2, concat_axis=3, tiled=True)  11.6 us
  transfers between devices with their start and end apart: 8, of which 7 were waited for; matrix products, arithmetic and copies ran while one was open for 3% of the time, Pallas kernels for 0%

commit v1 on v0

v1 whole, which is shorter than its diff:
```python
import math

import jax
import jax.numpy as jnp
import numpy as np
from jax import lax
from jax.experimental import pallas as pl
from jax.experimental.pallas import tpu as pltpu
from jax.sharding import PartitionSpec as P

f32 = jnp.float32
bf16 = jnp.bfloat16
BLOCKS = 64
SPAN = 256
HALF = 128
FILTERS = 32
GROUPS = 8
TAPS = 3
TOTAL = BLOCKS * SPAN


def split_table(values):
    high = values.astype(jnp.bfloat16)
    low = (values - high.astype(np.float64)).astype(jnp.bfloat16)
    return high, low


def tables():
    rows = np.arange(BLOCKS)
    cols = np.arange(SPAN)
    odd = 4 * rows + 1
    outer = 2 * math.pi * (odd[:, None] * rows[None, :] % 256) / 256.0
    g = np.concatenate([np.cos(outer), -np.sin(outer)], axis=0)
    g_high, g_low = split_table(g)
    forward_rows = np.concatenate([g_high, g_high, g_low], axis=1)
    t = g.T / TOTAL
    t_high, t_low = split_table(t)
    inverse_rows = np.concatenate([t_high, t_high, t_low], axis=1)
    inner = 2 * math.pi * (cols[:, None] * cols[None, :] % SPAN) / SPAN
    f = np.concatenate([np.cos(inner), np.sin(inner)], axis=1)
    f_high, f_low = split_table(f)
    turn = 2 * math.pi * (odd[:, None] * cols[None, :]) / (4.0 * TOTAL)
    turn = np.stack([np.cos(turn), np.sin(turn)]).astype(np.float32)
    return forward_rows, inverse_rows, f_high, f_low, turn


def halves(x):
    high = x.astype(bf16)
    return high, (x - high.astype(f32)).astype(bf16)


def dot(a, b):
    return jnp.dot(a, b, preferred_element_type=f32)


def dot_left(table, x):
    high, low = halves(x)
    return dot(table, jnp.concatenate([high, low, high], axis=0))


def dot_right(x, f_high, f_low):
    high, low = halves(x)
    return dot(high, f_high) + dot(low, f_high) + dot(high, f_low)


def later(x, n):
    row = lax.broadcasted_iota(jnp.int32, x.shape, 0)
    col = lax.broadcasted_iota(jnp.int32, x.shape, 1)
    here = pltpu.roll(x, n, 1)
    above = jnp.where(row == 0, 0.0, pltpu.roll(here, 1, 0))
    return jnp.where(col < n, above, here)


def sooner(x, n):
    row = lax.broadcasted_iota(jnp.int32, x.shape, 0)
    col = lax.broadcasted_iota(jnp.int32, x.shape, 1)
    here = pltpu.roll(x, SPAN - n, 1)
    below = jnp.where(row == BLOCKS - 1, 0.0, pltpu.roll(here, BLOCKS - 1, 0))
    return jnp.where(col >= SPAN - n, below, here)


def pack_kernel(inputs_ref, grad_ref, filters_ref, out_ref, rows_ref):
    h = filters_ref[...]
    h_high = h.astype(bf16).astype(f32)
    parts = [inputs_ref[b].astype(f32) for b in range(3)]
    parts += [grad_ref[...].astype(f32), h_high, h - h_high]
    rows_ref[...] = jnp.zeros_like(rows_ref)
    for i, part in enumerate(parts):
        for side in range(2):
            piece = part[:, side * HALF : (side + 1) * HALF]
            for copy in range(2):
                rows_ref[pl.ds(16 * copy + 2 * i + side, FILTERS, stride=32), :] = piece
    out_ref[...] = rows_ref[...].reshape(BLOCKS, 16, HALF).astype(bf16)


def spread(values, lanes):
    out = jnp.zeros((BLOCKS, HALF), f32)
    for i, value in enumerate(values):
        out = jnp.where(lanes == i, value, out)
    return out


def whole_sum(x):
    return jnp.sum(jnp.sum(x, axis=0, keepdims=True), axis=1, keepdims=True)


def channel_kernel(
    data_ref, taps_ref, skip_ref, left_ref, right_ref, f_high_ref, f_low_ref, turn_ref, out_ref, rows_ref
):
    place = lax.axis_index("seq")
    channel = place // 2
    rows_ref[...] = data_ref[...].astype(f32).reshape(BLOCKS * 16, HALF)

    def part(i):
        return jnp.concatenate(
            [rows_ref[pl.ds(2 * i + side, BLOCKS, stride=16), :] for side in range(2)], axis=1
        )

    branch = [part(b) for b in range(3)]
    grad = part(3)
    h_high, h_low = part(4), part(5)
    taps = [[taps_ref[b, j, channel] for j in range(TAPS)] for b in range(3)]
    direct = skip_ref[channel]
    moved = [[branch[b]] + [later(branch[b], j) for j in range(1, TAPS)] for b in range(3)]
    query, key, value = [
        taps[b][0] * moved[b][0] + taps[b][1] * moved[b][1] + taps[b][2] * moved[b][2]
        for b in range(3)
    ]
    product = key * value
    dw = grad * query

    cosine, sine = turn_ref[0], turn_ref[1]
    f_high, f_low = f_high_ref[...], f_low_ref[...]
    start = dot_left(left_ref[...], jnp.concatenate([product, dw, h_high + h_low], axis=1))
    stacked = []
    for i in range(3):
        re = start[:BLOCKS, i * SPAN : (i + 1) * SPAN]
        im = start[BLOCKS:, i * SPAN : (i + 1) * SPAN]
        stacked.append(re * cosine + im * sine)
        stacked.append(im * cosine - re * sine)
    spec = dot_right(jnp.concatenate(stacked, axis=0), f_high, f_low)

    def spectrum(i):
        re = spec[2 * i * BLOCKS : (2 * i + 1) * BLOCKS]
        im = spec[(2 * i + 1) * BLOCKS : (2 * i + 2) * BLOCKS]
        return re[:, :SPAN] + im[:, SPAN:], im[:, :SPAN] - re[:, SPAN:]

    (p_re, p_im), (d_re, d_im), (h_re, h_im) = [spectrum(i) for i in range(3)]
    joined = jnp.concatenate(
        [
            h_re * p_re - h_im * p_im,
            h_re * p_im + h_im * p_re,
            d_re * h_re + d_im * h_im,
            d_im * h_re - d_re * h_im,
            d_re * p_re + d_im * p_im,
            d_im * p_re - d_re * p_im,
        ],
        axis=0,
    )
    back = dot_right(joined, f_high, f_low)
    turned = []
    for i in range(3):
        re = back[2 * i * BLOCKS : (2 * i + 1) * BLOCKS]
        im = back[(2 * i + 1) * BLOCKS : (2 * i + 2) * BLOCKS]
        b_re = re[:, :SPAN] - im[:, SPAN:]
        b_im = im[:, :SPAN] + re[:, SPAN:]
        turned.append(
            jnp.concatenate([b_re * cosine - b_im * sine, b_im * cosine + b_re * sine], axis=0)
        )
    result = dot_left(right_ref[...], jnp.concatenate(turned, axis=1))
    conv_out = result[:, :SPAN] + direct * product
    dz = result[:, SPAN : 2 * SPAN] + direct * dw
    corr = result[:, 2 * SPAN :]

    grads = [grad * conv_out, dz * value, dz * key]
    side = lax.rem(place, 2)

    def mine(x):
        return jnp.where(side == 0, x[:, :HALF], x[:, HALF:])

    out_ref[...] = jnp.zeros_like(out_ref)
    for b in range(3):
        g = grads[b]
        total = taps[b][0] * g + taps[b][1] * sooner(g, 1) + taps[b][2] * sooner(g, 2)
        out_ref[pl.ds(b, BLOCKS, stride=8), :] = mine(total)
    out_ref[pl.ds(3, BLOCKS, stride=8), :] = mine(corr)
    sums = [whole_sum(grads[b] * moved[b][j]) for b in range(3) for j in range(TAPS)]
    sums.append(whole_sum(dw * product))
    lanes = lax.broadcasted_iota(jnp.int32, (BLOCKS, HALF), 1)
    out_ref[pl.ds(4, BLOCKS, stride=8), :] = spread(sums, lanes) * TOTAL**-0.5


def filter_kernel(data_ref, out_ref):
    out_ref[...] = data_ref[pl.ds(3, BLOCKS, stride=8), :].reshape(GROUPS, 8, HALF)


def place_kernel(data_ref, grads_ref, skip_ref, short_ref):
    for b in range(3):
        for side in range(2):
            grads_ref[b, :, side * HALF : (side + 1) * HALF] = data_ref[
                pl.ds(8 * side + b, FILTERS, stride=16), :
            ]
    sums = data_ref[pl.ds(4, FILTERS, stride=16), :]
    padded = jnp.concatenate([sums, jnp.zeros((HALF - FILTERS, HALF), f32)], axis=0)
    flipped = padded.T[:, :FILTERS]
    for b in range(3):
        short_ref[b] = flipped[TAPS * b : TAPS * (b + 1), :]
    skip_ref[...] = flipped[9:10, :]


def sum_kernel(data_ref, out_ref, rows_ref):
    total = data_ref[0]
    for i in range(1, GROUPS):
        total = total + data_ref[i]
    rows_ref[...] = total * (TOTAL * GROUPS) ** -0.5
    for side in range(2):
        out_ref[:, side * HALF : (side + 1) * HALF] = rows_ref[pl.ds(side, 4, stride=2), :]


vmem = pl.BlockSpec(memory_space=pltpu.VMEM)
smem = pl.BlockSpec(memory_space=pltpu.SMEM)
params = pltpu.CompilerParams(vmem_limit_bytes=32 * 1024 * 1024)


def like(shape, dtype=f32):
    return jax.ShapeDtypeStruct(shape, dtype)


def body(inputs, short_weights, filters, skip, grad_out):
    left, right, f_high, f_low, turn = [jnp.asarray(table) for table in tables()]
    message = pl.pallas_call(
        pack_kernel,
        out_shape=like((BLOCKS, 16, HALF), bf16),
        in_specs=[vmem] * 3,
        out_specs=vmem,
        scratch_shapes=[pltpu.VMEM((BLOCKS * 16, HALF), f32)],
        compiler_params=params,
    )(inputs, grad_out, filters)
    data = lax.all_to_all(message, "seq", split_axis=0, concat_axis=0, tiled=True)
    answer = pl.pallas_call(
        channel_kernel,
        out_shape=like((BLOCKS * 8, HALF)),
        in_specs=[vmem, smem, smem] + [vmem] * 5,
        out_specs=vmem,
        scratch_shapes=[pltpu.VMEM((BLOCKS * 16, HALF), f32)],
        compiler_params=params,
    )(data, short_weights, skip, left, right, f_high, f_low, turn)
    answer = lax.all_to_all(
        answer.reshape(BLOCKS, 8, HALF), "seq", split_axis=0, concat_axis=0, tiled=True
    ).reshape(BLOCKS * 8, HALF)
    partial = pl.pallas_call(
        filter_kernel,
        out_shape=like((GROUPS, 8, HALF)),
        in_specs=[vmem],
        out_specs=vmem,
        compiler_params=params,
    )(answer)
    partial = lax.all_to_all(partial, "chan", split_axis=0, concat_axis=0, tiled=True)
    grads, skip_grad, short_grad = pl.pallas_call(
        place_kernel,
        out_shape=(like((3, FILTERS, SPAN)), like((1, FILTERS)), like((3, TAPS, FILTERS))),
        in_specs=[vmem],
        out_specs=(vmem,) * 3,
        compiler_params=params,
    )(answer)
    filter_grad = pl.pallas_call(
        sum_kernel,
        out_shape=like((4, SPAN)),
        in_specs=[vmem],
        out_specs=vmem,
        scratch_shapes=[pltpu.VMEM((8, HALF), f32)],
        compiler_params=params,
    )(partial)
    return grads, filter_grad, skip_grad.reshape(FILTERS), short_grad


def solution(mesh):
    placed = (
        P(None, "chan", "seq"),
        P(None, None, "chan"),
        P(None, "seq"),
        P("chan"),
        P("chan", "seq"),
    )
    return jax.shard_map(
        body,
        mesh=mesh,
        in_specs=placed,
        out_specs=(P(None, "chan", "seq"), P("chan", "seq"), P("chan"), P(None, None, "chan")),
        check_vma=False,
    )
```

time: 432 us -> 74.8 us (0.17)
  the two profiles are of different devices: /device:TPU:64 before, /device:TPU:1 now
where the time goes in v1:
time: 74.8 us; the launch traced here: 74.4 us
  blocking collectives  55.4 us (74%)
  starting transfers between devices  6.63 us (9%)
  Pallas kernels  5.07 us (7%)
  waiting for transfers between devices  4.3 us (6%)
  local copies, waits for them, and re-layouts  2.3 us (3%)
    all_to_all x1, blocking collectives, body(): lax.all_to_all(message, 'seq', split_axis=0, concat_axis=0, tiled=True)  33.8 us
    all_to_all x1, blocking collectives, body(): lax.all_to_all(answer.reshape(BLOCKS, 8, HALF), 'seq', split_axis=0, conc...  21.6 us
    all_to_all x1, starting transfers between devices, body(): lax.all_to_all(partial, 'chan', split_axis=0, concat_axis=0, tiled=True)  6.63 us
    all_to_all x1, waiting for transfers between devices, body(): lax.all_to_all(partial, 'chan', split_axis=0, concat_axis=0, tiled=True)  4.3 us
    pallas_call x1, Pallas kernels, body(): pl.pallas_call(channel_kernel, out_shape=like((BLOCKS * 8, HALF)), in_spe...  2.81 us
    unnamed x20, local copies, waits for them, and re-layouts  2.3 us
  transfers between devices with their start and end apart: 1, of which 1 were waited for; matrix products, arithmetic and copies ran while one was open for 0% of the time, Pallas kernels for 1%

profile of v1, /device:TPU:1, one launch (start us, length us, event | category | flops | bytes accessed | tf_op | source)
XLA Modules:
  0.0 74.4 jit_solution(3269866939440591599)
XLA Ops:
  0.6 0.0 copy-start.5
  0.6 0.8 %copy-done.5 = bf16[3,32,256]{2,1,0:T(8,128)(2,1)S(1)} copy-done((bf16[3,32,256]{2,1,0:T(8,128)(2,1)S(1)}, bf16[3,32,256]{2,1,0:T(8,128)(2,1)}, u32[]{:S(2)}) %copy-start.5) | copy-done | bytes 49176
  1.4 0.0 copy-start.6
  1.4 0.8 %copy-done.6 = f32[32,256]{1,0:T(8,128)S(1)} copy-done((f32[32,256]{1,0:T(8,128)S(1)}, f32[32,256]{1,0:T(8,128)}, u32[]{:S(2)}) %copy-start.6) | copy-done | bytes 32792
  2.2 0.0 copy-start.7
  2.2 0.7 copy-done.7
  2.9 0.0 copy-start.2
  2.9 0.0 copy-start.3
  2.9 0.0 copy-start.4
  2.9 0.0 copy-start.8
  2.9 0.0 copy-start.9
  2.9 0.3 shard_map.129
  3.3 0.0 copy-start
  3.3 0.0 copy-start.1
  3.3 33.8 %all_to_all.15.data_ref = bf16[64,16,128]{2,1,0:T(8,128)(2,1)S(1)} all-to-all(bf16[64,16,128]{2,1,0:T(8,128)(2,1)S(1)} %shard_map.129), channel_id=1, replica_groups=mesh['seq'=64,'chan'=8] {'seq'}, dimensions={0} | all-to-all | bytes 524288 | tf_op jit(solution)/shard_map/all_to_all | solution.py:239
  37.1 0.0 copy-done.2
  37.1 0.0 copy-done.3
  37.1 0.0 copy-done.4
  37.1 0.0 copy-done.8
  37.1 0.0 copy-done.9
  37.1 0.0 copy-done
  37.1 0.0 copy-done.1
  37.1 2.8 %shard_map.130 = f32[512,128]{1,0:T(8,128)S(1)} custom-call(bf16[64,16,128]{2,1,0:T(8,128)(2,1)S(1)} %all_to_all.15.data_ref, f32[3,3,32]{2,1,0:T(4,128)S(1)} %copy-done.8, f32[32]{0:T(128)S(1)} %copy-done.9, bf16[128,192]{1,0:T(8,128)(2,1)S(1)} %copy-done.3, bf16[64,384]{1,0:T(8,128)(2,1)S(1)} %copy-done.4, bf16[256,512]{1,0:T(8,128)(2,1)S(1)} %copy-done.1, ...), custom_call_target="tpu_custom_call" | custom-call | tf_op jit(solution)/shard_map/pallas_call | solution.py:240
  40.0 21.6 %all_to_all.16 = f32[64,8,128]{2,1,0:T(8,128)S(1)} all-to-all(f32[64,8,128]{2,1,0:T(8,128)S(1)} %bitcast.5), channel_id=1, replica_groups=mesh['seq'=64,'chan'=8] {'seq'}, dimensions={0} | all-to-all | bytes 524288 | tf_op jit(solution)/shard_map/all_to_all | solution.py:248
  61.6 0.6 shard_map.132
  62.2 6.6 %all-to-all-start.2 = ((f32[8,8,128]{2,1,0:T(8,128)}), f32[8,8,128]{2,1,0:T(8,128)S(1)}, u32[]{:S(2)}, u32[]{:S(2)}) async-start(f32[8,8,128]{2,1,0:T(8,128)} %shard_map.132), calls=%async_computation.2 | async-start | bytes 65536 | tf_op jit(solution)/shard_map/all_to_all | solution.py:258
  68.8 0.7 shard_map.131
  69.5 4.3 %all-to-all-done.2.data_ref = f32[8,8,128]{2,1,0:T(8,128)S(1)} async-done(((f32[8,8,128]{2,1,0:T(8,128)}), f32[8,8,128]{2,1,0:T(8,128)S(1)}, u32[]{:S(2)}, u32[]{:S(2)}) %all-to-all-start.2) | async-done | bytes 32800 | tf_op jit(solution)/shard_map/all_to_all | solution.py:258
  73.8 0.6 shard_map.133
Async XLA Ops:
  0.6 0.8 %copy-start.5 = (bf16[3,32,256]{2,1,0:T(8,128)(2,1)S(1)}, bf16[3,32,256]{2,1,0:T(8,128)(2,1)}, u32[]{:S(2)}) copy-start(bf16[3,32,256]{2,1,0:T(8,128)(2,1)} %inputs_ref.1) | copy-start | bytes 147460
  1.4 0.8 %copy-start.6 = (f32[32,256]{1,0:T(8,128)S(1)}, f32[32,256]{1,0:T(8,128)}, u32[]{:S(2)}) copy-start(f32[32,256]{1,0:T(8,128)} %filters_ref.1) | copy-start | bytes 98308
  2.2 0.7 copy-start.7
  2.9 34.2 %copy-start.2 = (f32[2,64,256]{2,1,0:T(8,128)S(1)}, f32[2,64,256]{2,1,0:T(8,128)}, u32[]{:S(2)}) copy-start(f32[2,64,256]{2,1,0:T(8,128)} %constant.14.clone.turn_ref) | copy-start | bytes 393220
  2.9 34.2 %copy-start.3 = (bf16[128,192]{1,0:T(8,128)(2,1)S(1)}, bf16[128,192]{1,0:T(8,128)(2,1)}, u32[]{:S(2)}) copy-start(bf16[128,192]{1,0:T(8,128)(2,1)} %constant.10.clone.left_ref) | copy-start | bytes 147460
  2.9 34.2 %copy-start.4 = (bf16[64,384]{1,0:T(8,128)(2,1)S(1)}, bf16[64,384]{1,0:T(8,128)(2,1)}, u32[]{:S(2)}) copy-start(bf16[64,384]{1,0:T(8,128)(2,1)} %constant.11.clone.right_ref) | copy-start | bytes 147460
  2.9 34.2 %copy-start.8 = (f32[3,3,32]{2,1,0:T(4,128)S(1)}, f32[3,3,32]{2,1,0:T(4,128)}, u32[]{:S(2)}) copy-start(f32[3,3,32]{2,1,0:T(4,128)} %taps_ref.1) | copy-start | bytes 3460
  2.9 34.2 %copy-start.9 = (f32[32]{0:T(128)S(1)}, f32[32]{0:T(128)}, u32[]{:S(2)}) copy-start(f32[32]{0:T(128)} %skip_ref.1) | copy-start | bytes 388
  3.3 33.8 %copy-start = (bf16[256,512]{1,0:T(8,128)(2,1)S(1)}, bf16[256,512]{1,0:T(8,128)(2,1)}, u32[]{:S(2)}) copy-start(bf16[256,512]{1,0:T(8,128)(2,1)} %constant.13.clone.f_low_ref) | copy-start | bytes 786436
  3.3 33.8 %copy-start.1 = (bf16[256,512]{1,0:T(8,128)(2,1)S(1)}, bf16[256,512]{1,0:T(8,128)(2,1)}, u32[]{:S(2)}) copy-start(bf16[256,512]{1,0:T(8,128)(2,1)} %constant.12.clone.f_high_ref) | copy-start | bytes 786436
  62.2 11.6 %all-to-all-start.2 = ((f32[8,8,128]{2,1,0:T(8,128)}), f32[8,8,128]{2,1,0:T(8,128)S(1)}, u32[]{:S(2)}, u32[]{:S(2)}) async-start(f32[8,8,128]{2,1,0:T(8,128)} %shard_map.132), calls=%async_computation.2 | async-start | bytes 65536 | tf_op jit(solution)/shard_map/all_to_all | solution.py:258

commit v2 on v1

--- a/solution.py
+++ b/solution.py
@@ -16,6 +16,7 @@
 FILTERS = 32
 GROUPS = 8
 TAPS = 3
+ROWS = 5
 TOTAL = BLOCKS * SPAN
 
 
@@ -49,6 +50,10 @@
     return high, (x - high.astype(f32)).astype(bf16)
 
 
+def place_of(i):
+    return i % 4, slice(i // 4 * HALF, (i // 4 + 1) * HALF)
+
+
 def dot(a, b):
     return jnp.dot(a, b, preferred_element_type=f32)
 
@@ -79,25 +84,28 @@
     return jnp.where(col >= SPAN - n, below, here)
 
 
-def pack_kernel(inputs_ref, grad_ref, filters_ref, out_ref, rows_ref):
+def pack_kernel(inputs_hbm, grad_hbm, filters_hbm, out_ref, inputs_ref, grad_ref, filters_ref, rows_ref, sems):
+    copies = [
+        pltpu.make_async_copy(source, target, sems.at[i])
+        for i, (source, target) in enumerate(
+            [(inputs_hbm, inputs_ref), (grad_hbm, grad_ref), (filters_hbm, filters_ref)]
+        )
+    ]
+    for copy in copies:
+        copy.start()
+    for copy in copies:
+        copy.wait()
     h = filters_ref[...]
     h_high = h.astype(bf16).astype(f32)
     parts = [inputs_ref[b].astype(f32) for b in range(3)]
     parts += [grad_ref[...].astype(f32), h_high, h - h_high]
-    rows_ref[...] = jnp.zeros_like(rows_ref)
     for i, part in enumerate(parts):
         for side in range(2):
             piece = part[:, side * HALF : (side + 1) * HALF]
+            row, tile = place_of(2 * i + side)
             for copy in range(2):
-                rows_ref[pl.ds(16 * copy + 2 * i + side, FILTERS, stride=32), :] = piece
-    out_ref[...] = rows_ref[...].reshape(BLOCKS, 16, HALF).astype(bf16)
-
-
-def spread(values, lanes):
-    out = jnp.zeros((BLOCKS, HALF), f32)
-    for i, value in enumerate(values):
-        out = jnp.where(lanes == i, value, out)
-    return out
+                rows_ref[copy * FILTERS : (copy + 1) * FILTERS, row, tile] = piece
+    out_ref[...] = rows_ref[...].astype(bf16)
 
 
 def whole_sum(x):
@@ -108,13 +116,15 @@
     data_ref, taps_ref, skip_ref, left_ref, right_ref, f_high_ref, f_low_ref, turn_ref, out_ref, rows_ref
 ):
     place = lax.axis_index("seq")
-    channel = place // 2
-    rows_ref[...] = data_ref[...].astype(f32).reshape(BLOCKS * 16, HALF)
+    channel = lax.rem(place, FILTERS)
+    rows_ref[...] = data_ref[...].astype(f32)
 
     def part(i):
-        return jnp.concatenate(
-            [rows_ref[pl.ds(2 * i + side, BLOCKS, stride=16), :] for side in range(2)], axis=1
-        )
+        pieces = []
+        for side in range(2):
+            row, tile = place_of(2 * i + side)
+            pieces.append(rows_ref[:, row, tile])
+        return jnp.concatenate(pieces, axis=1)
 
     branch = [part(b) for b in range(3)]
     grad = part(3)
@@ -173,53 +183,57 @@
     corr = result[:, 2 * SPAN :]
 
     grads = [grad * conv_out, dz * value, dz * key]
-    side = lax.rem(place, 2)
+    side = place // FILTERS
 
     def mine(x):
         return jnp.where(side == 0, x[:, :HALF], x[:, HALF:])
 
-    out_ref[...] = jnp.zeros_like(out_ref)
     for b in range(3):
         g = grads[b]
         total = taps[b][0] * g + taps[b][1] * sooner(g, 1) + taps[b][2] * sooner(g, 2)
-        out_ref[pl.ds(b, BLOCKS, stride=8), :] = mine(total)
-    out_ref[pl.ds(3, BLOCKS, stride=8), :] = mine(corr)
+        out_ref[pl.ds(b, BLOCKS, stride=ROWS), :] = mine(total)
+    out_ref[pl.ds(3, BLOCKS, stride=ROWS), :] = mine(corr)
     sums = [whole_sum(grads[b] * moved[b][j]) for b in range(3) for j in range(TAPS)]
     sums.append(whole_sum(dw * product))
-    lanes = lax.broadcasted_iota(jnp.int32, (BLOCKS, HALF), 1)
-    out_ref[pl.ds(4, BLOCKS, stride=8), :] = spread(sums, lanes) * TOTAL**-0.5
+    lanes = lax.broadcasted_iota(jnp.int32, (1, HALF), 1)
+    line = jnp.zeros((1, HALF), f32)
+    for i, value in enumerate(sums):
+        line = jnp.where(lanes == i, value, line)
+    out_ref[pl.ds(4, BLOCKS, stride=ROWS), :] = jnp.broadcast_to(line * TOTAL**-0.5, (BLOCKS, HALF))
 
 
 def filter_kernel(data_ref, out_ref):
-    out_ref[...] = data_ref[pl.ds(3, BLOCKS, stride=8), :].reshape(GROUPS, 8, HALF)
-
-
-def place_kernel(data_ref, grads_ref, skip_ref, short_ref):
+    for group in range(GROUPS):
+        for side in range(2):
+            first = ROWS * (FILTERS * side + 4 * group) + 3
+            out_ref[group, 4 * side : 4 * side + 4, :] = data_ref[pl.ds(first, 4, stride=ROWS), :]
+
+
+def place_kernel(data_ref, partial_ref, grads_ref, skip_ref, short_ref, filter_ref):
     for b in range(3):
         for side in range(2):
             grads_ref[b, :, side * HALF : (side + 1) * HALF] = data_ref[
-                pl.ds(8 * side + b, FILTERS, stride=16), :
+                pl.ds(ROWS * FILTERS * side + b, FILTERS, stride=ROWS), :
             ]
-    sums = data_ref[pl.ds(4, FILTERS, stride=16), :]
+    sums = data_ref[pl.ds(4, FILTERS, stride=ROWS), :]
     padded = jnp.concatenate([sums, jnp.zeros((HALF - FILTERS, HALF), f32)], axis=0)
     flipped = padded.T[:, :FILTERS]
     for b in range(3):
         short_ref[b] = flipped[TAPS * b : TAPS * (b + 1), :]
     skip_ref[...] = flipped[9:10, :]
-
-
-def sum_kernel(data_ref, out_ref, rows_ref):
-    total = data_ref[0]
+    total = partial_ref[0]
     for i in range(1, GROUPS):
-        total = total + data_ref[i]
-    rows_ref[...] = total * (TOTAL * GROUPS) ** -0.5
+        total = total + partial_ref[i]
+    total = total * (TOTAL * GROUPS) ** -0.5
     for side in range(2):
-        out_ref[:, side * HALF : (side + 1) * HALF] = rows_ref[pl.ds(side, 4, stride=2), :]
+        filter_ref[:, side * HALF : (side + 1) * HALF] = total[4 * side : 4 * side + 4, :]
 
 
 vmem = pl.BlockSpec(memory_space=pltpu.VMEM)
+hbm = pl.BlockSpec(memory_space=pltpu.HBM)
 smem = pl.BlockSpec(memory_space=pltpu.SMEM)
 params = pltpu.CompilerParams(vmem_limit_bytes=32 * 1024 * 1024)
+pack_params = pltpu.CompilerParams(vmem_limit_bytes=56 * 1024 * 1024)
 
 
 def like(shape, dtype=f32):
@@ -230,24 +244,30 @@
     left, right, f_high, f_low, turn = [jnp.asarray(table) for table in tables()]
     message = pl.pallas_call(
         pack_kernel,
-        out_shape=like((BLOCKS, 16, HALF), bf16),
-        in_specs=[vmem] * 3,
+        out_shape=like((BLOCKS, 4, 3 * HALF), bf16),
+        in_specs=[hbm] * 3,
         out_specs=vmem,
-        scratch_shapes=[pltpu.VMEM((BLOCKS * 16, HALF), f32)],
-        compiler_params=params,
+        scratch_shapes=[
+            pltpu.VMEM((3, FILTERS, SPAN), bf16),
+            pltpu.VMEM((FILTERS, SPAN), bf16),
+            pltpu.VMEM((FILTERS, SPAN), f32),
+            pltpu.VMEM((BLOCKS, 4, 3 * HALF), f32),
+            pltpu.SemaphoreType.DMA((3,)),
+        ],
+        compiler_params=pack_params,
     )(inputs, grad_out, filters)
     data = lax.all_to_all(message, "seq", split_axis=0, concat_axis=0, tiled=True)
     answer = pl.pallas_call(
         channel_kernel,
-        out_shape=like((BLOCKS * 8, HALF)),
+        out_shape=like((BLOCKS * ROWS, HALF)),
         in_specs=[vmem, smem, smem] + [vmem] * 5,
         out_specs=vmem,
-        scratch_shapes=[pltpu.VMEM((BLOCKS * 16, HALF), f32)],
+        scratch_shapes=[pltpu.VMEM((BLOCKS, 4, 3 * HALF), f32)],
         compiler_params=params,
     )(data, short_weights, skip, left, right, f_high, f_low, turn)
     answer = lax.all_to_all(
-        answer.reshape(BLOCKS, 8, HALF), "seq", split_axis=0, concat_axis=0, tiled=True
-    ).reshape(BLOCKS * 8, HALF)
+        answer.reshape(BLOCKS, 1, ROWS * HALF), "seq", split_axis=0, concat_axis=0, tiled=True
+    ).reshape(BLOCKS * ROWS, HALF)
     partial = pl.pallas_call(
         filter_kernel,
         out_shape=like((GROUPS, 8, HALF)),
@@ -256,21 +276,18 @@
         compiler_params=params,
     )(answer)
     partial = lax.all_to_all(partial, "chan", split_axis=0, concat_axis=0, tiled=True)
-    grads, skip_grad, short_grad = pl.pallas_call(
+    grads, skip_grad, short_grad, filter_grad = pl.pallas_call(
         place_kernel,
-        out_shape=(like((3, FILTERS, SPAN)), like((1, FILTERS)), like((3, TAPS, FILTERS))),
-        in_specs=[vmem],
-        out_specs=(vmem,) * 3,
+        out_shape=(
+            like((3, FILTERS, SPAN)),
+            like((1, FILTERS)),
+            like((3, TAPS, FILTERS)),
+            like((4, SPAN)),
+        ),
+        in_specs=[vmem] * 2,
+        out_specs=(vmem,) * 4,
         compiler_params=params,
-    )(answer)
-    filter_grad = pl.pallas_call(
-        sum_kernel,
-        out_shape=like((4, SPAN)),
-        in_specs=[vmem],
-        out_specs=vmem,
-        scratch_shapes=[pltpu.VMEM((8, HALF), f32)],
-        compiler_params=params,
-    )(partial)
+    )(answer, partial)
     return grads, filter_grad, skip_grad.reshape(FILTERS), short_grad
 
 

time: 74.8 us -> 71.8 us (0.960)
  blocking collectives: 55.4 us -> 63.6 us
  starting transfers between devices: 6.63 us -> 0 us
  waiting for transfers between devices: 4.3 us -> 0 us
    all_to_all x1 -> x2, blocking collectives: 21.6 us -> 29.9 us  [the longest x1 19.9 us: body(): lax.all_to_all(answer.reshape(BLOCKS, 1, ROWS * HALF), 'seq', split_axis=...]
    all_to_all x1 -> x0, starting transfers between devices: 6.63 us -> none  [body(): lax.all_to_all(partial, 'chan', split_axis=0, concat_axis=0, tiled=True)]
    all_to_all x1 -> x0, waiting for transfers between devices: 4.3 us -> none  [body(): lax.all_to_all(partial, 'chan', split_axis=0, concat_axis=0, tiled=True)]
    pallas_call x3 -> x2, Pallas kernels: 3.77 us -> 4.73 us  [the longest x1 2.92 us: body(): pl.pallas_call(channel_kernel, out_shape=like((BLOCKS * ROWS, HALF)), in_...]
    unnamed x20 -> x14, local copies, waits for them, and re-layouts: 2.3 us -> 1.66 us
  transfers between devices with their start and end apart: 1 -> 0, of which waited for: 1 -> 0; matrix products, arithmetic and copies ran while one was open for 0% -> 0% of each run, Pallas kernels for 1% -> 0%
where the time goes in v2:
time: 71.8 us; the launch traced here: 71.4 us
  blocking collectives  63.6 us (89%)
  Pallas kernels  5.41 us (8%)
  local copies, waits for them, and re-layouts  1.66 us (2%)
    all_to_all x1, blocking collectives, body(): lax.all_to_all(message, 'seq', split_axis=0, concat_axis=0, tiled=True)  33.7 us
    all_to_all x1, blocking collectives, body(): lax.all_to_all(answer.reshape(BLOCKS, 1, ROWS * HALF), 'seq', split_axis=...  19.9 us
    all_to_all x1, blocking collectives, body(): lax.all_to_all(partial, 'chan', split_axis=0, concat_axis=0, tiled=True)  10 us
    pallas_call x1, Pallas kernels, body(): pl.pallas_call(channel_kernel, out_shape=like((BLOCKS * ROWS, HALF)), in_...  2.92 us
    pallas_call x1, Pallas kernels, body(): pl.pallas_call(pack_kernel, out_shape=like((BLOCKS, 4, 3 * HALF), bf16),...  1.82 us
    unnamed x14, local copies, waits for them, and re-layouts  1.66 us

profile of v2, /device:TPU:1, one launch (start us, length us, event | category | flops | bytes accessed | tf_op | source)
XLA Modules:
  0.0 71.4 jit_solution(1877829243890486878)
XLA Ops:
  0.6 0.0 copy-start.1
  0.6 0.0 copy-start.5
  0.7 0.0 copy-start.6
  0.7 1.8 %shard_map.129 = bf16[64,4,384]{2,1,0:T(4,128)(2,1)} custom-call(bf16[3,32,256]{2,1,0:T(8,128)(2,1)} %inputs_hbm.1, bf16[32,256]{1,0:T(8,128)(2,1)} %grad_hbm.1, f32[32,256]{1,0:T(8,128)} %filters_hbm.1), custom_call_target="tpu_custom_call" | custom-call | tf_op jit(solution)/shard_map/pallas_call | solution.py:245
  2.5 0.0 copy-start
  2.5 0.0 copy-start.2
  2.5 33.7 %all_to_all.15.data_ref = bf16[64,4,384]{2,1,0:T(4,128)(2,1)S(1)} all-to-all(bf16[64,4,384]{2,1,0:T(4,128)(2,1)} %shard_map.129), channel_id=1, replica_groups=mesh['seq'=64,'chan'=8] {'seq'}, dimensions={0} | all-to-all | bytes 393216 | tf_op jit(solution)/shard_map/all_to_all | solution.py:259
  36.2 0.0 copy-done.1
  36.2 0.0 copy-done.5
  36.2 0.0 copy-done.6
  36.2 0.0 copy-done
  36.2 0.0 copy-done.2
  36.2 0.0 copy-start.3
  36.2 0.8 %copy-done.3 = bf16[128,192]{1,0:T(8,128)(2,1)S(1)} copy-done((bf16[128,192]{1,0:T(8,128)(2,1)S(1)}, bf16[128,192]{1,0:T(8,128)(2,1)}, u32[]{:S(2)}) %copy-start.3) | copy-done | bytes 49176
  37.1 0.0 copy-start.4
  37.1 0.8 %copy-done.4 = bf16[64,384]{1,0:T(8,128)(2,1)S(1)} copy-done((bf16[64,384]{1,0:T(8,128)(2,1)S(1)}, bf16[64,384]{1,0:T(8,128)(2,1)}, u32[]{:S(2)}) %copy-start.4) | copy-done | bytes 49176
  37.9 2.9 %shard_map.130 = f32[320,128]{1,0:T(8,128)S(1)} custom-call(bf16[64,4,384]{2,1,0:T(4,128)(2,1)S(1)} %all_to_all.15.data_ref, f32[3,3,32]{2,1,0:T(4,128)S(1)} %copy-done.5, f32[32]{0:T(128)S(1)} %copy-done.6, bf16[128,192]{1,0:T(8,128)(2,1)S(1)} %copy-done.3, bf16[64,384]{1,0:T(8,128)(2,1)S(1)} %copy-done.4, bf16[256,512]{1,0:T(8,128)(2,1)S(1)} %copy-done.1, ...), custom_call_target="tpu_custom_call" | custom-call | tf_op jit(solution)/shard_map/pallas_call | solution.py:260
  40.8 19.9 %all_to_all.16 = f32[64,1,640]{2,1,0:T(1,128)S(1)} all-to-all(f32[64,1,640]{2,1,0:T(1,128)S(1)} %bitcast.5), channel_id=1, replica_groups=mesh['seq'=64,'chan'=8] {'seq'}, dimensions={0} | all-to-all | bytes 327680 | tf_op jit(solution)/shard_map/all_to_all | solution.py:268
  60.7 10.0 %all_to_all.17.partial_ref = f32[8,8,128]{2,1,0:T(8,128)S(1)} all-to-all(f32[8,8,128]{2,1,0:T(8,128)S(1)} %shard_map.131), channel_id=1, replica_groups=mesh['seq'=64,'chan'=8] {'chan'}, dimensions={0} | all-to-all | bytes 65536 | tf_op jit(solution)/shard_map/all_to_all | solution.py:278
  70.7 0.7 shard_map.132
  (1 shorter events, 0.0 us)
Async XLA Ops:
  0.6 35.6 %copy-start.1 = (bf16[256,512]{1,0:T(8,128)(2,1)S(1)}, bf16[256,512]{1,0:T(8,128)(2,1)}, u32[]{:S(2)}) copy-start(bf16[256,512]{1,0:T(8,128)(2,1)} %constant.12.clone.f_high_ref) | copy-start | bytes 786436
  0.6 35.6 %copy-start.5 = (f32[3,3,32]{2,1,0:T(4,128)S(1)}, f32[3,3,32]{2,1,0:T(4,128)}, u32[]{:S(2)}) copy-start(f32[3,3,32]{2,1,0:T(4,128)} %taps_ref.1) | copy-start | bytes 3460
  0.7 35.5 %copy-start.6 = (f32[32]{0:T(128)S(1)}, f32[32]{0:T(128)}, u32[]{:S(2)}) copy-start(f32[32]{0:T(128)} %skip_ref.1) | copy-start | bytes 388
  2.5 33.7 %copy-start = (bf16[256,512]{1,0:T(8,128)(2,1)S(1)}, bf16[256,512]{1,0:T(8,128)(2,1)}, u32[]{:S(2)}) copy-start(bf16[256,512]{1,0:T(8,128)(2,1)} %constant.13.clone.f_low_ref) | copy-start | bytes 786436
  2.5 33.7 %copy-start.2 = (f32[2,64,256]{2,1,0:T(8,128)S(1)}, f32[2,64,256]{2,1,0:T(8,128)}, u32[]{:S(2)}) copy-start(f32[2,64,256]{2,1,0:T(8,128)} %constant.14.clone.turn_ref) | copy-start | bytes 393220
  36.2 0.8 %copy-start.3 = (bf16[128,192]{1,0:T(8,128)(2,1)S(1)}, bf16[128,192]{1,0:T(8,128)(2,1)}, u32[]{:S(2)}) copy-start(bf16[128,192]{1,0:T(8,128)(2,1)} %constant.10.clone.left_ref) | copy-start | bytes 147460
  37.1 0.8 %copy-start.4 = (bf16[64,384]{1,0:T(8,128)(2,1)S(1)}, bf16[64,384]{1,0:T(8,128)(2,1)}, u32[]{:S(2)}) copy-start(bf16[64,384]{1,0:T(8,128)(2,1)} %constant.11.clone.right_ref) | copy-start | bytes 147460

commit v3 on v2

--- a/solution.py
+++ b/solution.py
@@ -36,13 +36,19 @@
     forward_rows = np.concatenate([g_high, g_high, g_low], axis=1)
     t = g.T / TOTAL
     t_high, t_low = split_table(t)
-    inverse_rows = np.concatenate([t_high, t_high, t_low], axis=1)
+    inverse_rows = np.concatenate([t_high, t_low], axis=1)
     inner = 2 * math.pi * (cols[:, None] * cols[None, :] % SPAN) / SPAN
     f = np.concatenate([np.cos(inner), np.sin(inner)], axis=1)
     f_high, f_low = split_table(f)
-    turn = 2 * math.pi * (odd[:, None] * cols[None, :]) / (4.0 * TOTAL)
-    turn = np.stack([np.cos(turn), np.sin(turn)]).astype(np.float32)
-    return forward_rows, inverse_rows, f_high, f_low, turn
+    strip = np.zeros((3 * BLOCKS, SPAN), dtype=jnp.bfloat16)
+    strip[: 2 * BLOCKS, : 3 * BLOCKS] = forward_rows
+    strip[2 * BLOCKS :] = inverse_rows
+    eight = np.arange(8)
+    coarse = 2 * math.pi * (32 * eight[:, None] * cols[None, :]) / (4.0 * TOTAL)
+    fine = 2 * math.pi * ((4 * eight + 1)[:, None] * cols[None, :]) / (4.0 * TOTAL)
+    turn = np.concatenate([np.cos(coarse), np.sin(coarse), np.cos(fine), np.sin(fine)])
+    turn = turn.astype(np.float32)
+    return f_high, f_low, strip, turn
 
 
 def halves(x):
@@ -112,8 +118,18 @@
     return jnp.sum(jnp.sum(x, axis=0, keepdims=True), axis=1, keepdims=True)
 
 
+def turns(turn_ref):
+    cosines, sines = [], []
+    fine_cos, fine_sin = turn_ref[16:24, :], turn_ref[24:32, :]
+    for a in range(8):
+        coarse_cos, coarse_sin = turn_ref[a : a + 1, :], turn_ref[8 + a : 9 + a, :]
+        cosines.append(coarse_cos * fine_cos - coarse_sin * fine_sin)
+        sines.append(coarse_sin * fine_cos + coarse_cos * fine_sin)
+    return jnp.concatenate(cosines, axis=0), jnp.concatenate(sines, axis=0)
+
+
 def channel_kernel(
-    data_ref, taps_ref, skip_ref, left_ref, right_ref, f_high_ref, f_low_ref, turn_ref, out_ref, rows_ref
+    data_ref, taps_ref, skip_ref, high_ref, low_ref, strip_ref, turn_ref, out_ref, rows_ref
 ):
     place = lax.axis_index("seq")
     channel = lax.rem(place, FILTERS)
@@ -139,9 +155,12 @@
     product = key * value
     dw = grad * query
 
-    cosine, sine = turn_ref[0], turn_ref[1]
-    f_high, f_low = f_high_ref[...], f_low_ref[...]
-    start = dot_left(left_ref[...], jnp.concatenate([product, dw, h_high + h_low], axis=1))
+    cosine, sine = turns(turn_ref)
+    f_high, f_low = high_ref[...], low_ref[...]
+    left = strip_ref[: 2 * BLOCKS, : 3 * BLOCKS]
+    right = strip_ref[2 * BLOCKS :, :]
+    right = jnp.concatenate([right[:, :HALF], right], axis=1)
+    start = dot_left(left, jnp.concatenate([product, dw, h_high + h_low], axis=1))
     stacked = []
     for i in range(3):
         re = start[:BLOCKS, i * SPAN : (i + 1) * SPAN]
@@ -177,7 +196,7 @@
         turned.append(
             jnp.concatenate([b_re * cosine - b_im * sine, b_im * cosine + b_re * sine], axis=0)
         )
-    result = dot_left(right_ref[...], jnp.concatenate(turned, axis=1))
+    result = dot_left(right, jnp.concatenate(turned, axis=1))
     conv_out = result[:, :SPAN] + direct * product
     dz = result[:, SPAN : 2 * SPAN] + direct * dw
     corr = result[:, 2 * SPAN :]
@@ -241,7 +260,7 @@
 
 
 def body(inputs, short_weights, filters, skip, grad_out):
-    left, right, f_high, f_low, turn = [jnp.asarray(table) for table in tables()]
+    f_high, f_low, strip, turn = [jnp.asarray(values) for values in tables()]
     message = pl.pallas_call(
         pack_kernel,
         out_shape=like((BLOCKS, 4, 3 * HALF), bf16),
@@ -260,11 +279,11 @@
     answer = pl.pallas_call(
         channel_kernel,
         out_shape=like((BLOCKS * ROWS, HALF)),
-        in_specs=[vmem, smem, smem] + [vmem] * 5,
+        in_specs=[vmem, smem, smem] + [vmem] * 4,
         out_specs=vmem,
         scratch_shapes=[pltpu.VMEM((BLOCKS, 4, 3 * HALF), f32)],
         compiler_params=params,
-    )(data, short_weights, skip, left, right, f_high, f_low, turn)
+    )(data, short_weights, skip, f_high, f_low, strip, turn)
     answer = lax.all_to_all(
         answer.reshape(BLOCKS, 1, ROWS * HALF), "seq", split_axis=0, concat_axis=0, tiled=True
     ).reshape(BLOCKS * ROWS, HALF)

time: 71.8 us -> 70 us (0.975)
  local copies, waits for them, and re-layouts: 1.66 us -> 0.04 us
    unnamed x14 -> x12, local copies, waits for them, and re-layouts: 1.66 us -> 0.04 us
where the time goes in v3:
time: 70 us; the launch traced here: 69.8 us
  blocking collectives  63.6 us (91%)
  Pallas kernels  5.41 us (8%)
  between operations  0.72 us (1%)
    all_to_all x1, blocking collectives, body(): lax.all_to_all(message, 'seq', split_axis=0, concat_axis=0, tiled=True)  33.7 us
    all_to_all x1, blocking collectives, body(): lax.all_to_all(answer.reshape(BLOCKS, 1, ROWS * HALF), 'seq', split_axis=...  19.9 us
    all_to_all x1, blocking collectives, body(): lax.all_to_all(partial, 'chan', split_axis=0, concat_axis=0, tiled=True)  10 us
    pallas_call x1, Pallas kernels, body(): pl.pallas_call(channel_kernel, out_shape=like((BLOCKS * ROWS, HALF)), in_...  2.92 us
    pallas_call x1, Pallas kernels, body(): pl.pallas_call(pack_kernel, out_shape=like((BLOCKS, 4, 3 * HALF), bf16),...  1.81 us

profile of v3, /device:TPU:1, one launch (start us, length us, event | category | flops | bytes accessed | tf_op | source)
XLA Modules:
  0.0 69.8 jit_solution(18236084995094913420)
XLA Ops:
  0.6 0.0 copy-start.1
  0.6 0.0 copy-start.4
  0.7 0.0 copy-start.5
  0.7 1.8 %shard_map.120 = bf16[64,4,384]{2,1,0:T(4,128)(2,1)} custom-call(bf16[3,32,256]{2,1,0:T(8,128)(2,1)} %inputs_hbm.1, bf16[32,256]{1,0:T(8,128)(2,1)} %grad_hbm.1, f32[32,256]{1,0:T(8,128)} %filters_hbm.1), custom_call_target="tpu_custom_call" | custom-call | tf_op jit(solution)/shard_map/pallas_call | solution.py:264
  2.5 0.0 copy-start
  2.5 0.0 copy-start.2
  2.5 0.0 copy-start.3
  2.5 33.7 %all_to_all.15.data_ref = bf16[64,4,384]{2,1,0:T(4,128)(2,1)S(1)} all-to-all(bf16[64,4,384]{2,1,0:T(4,128)(2,1)} %shard_map.120), channel_id=1, replica_groups=mesh['seq'=64,'chan'=8] {'seq'}, dimensions={0} | all-to-all | bytes 393216 | tf_op jit(solution)/shard_map/all_to_all | solution.py:278
  36.2 0.0 copy-done.1
  36.2 0.0 copy-done.4
  36.2 0.0 copy-done.5
  36.2 0.0 copy-done
  36.2 0.0 copy-done.2
  36.2 0.0 copy-done.3
  36.2 2.9 %shard_map.121 = f32[320,128]{1,0:T(8,128)S(1)} custom-call(bf16[64,4,384]{2,1,0:T(4,128)(2,1)S(1)} %all_to_all.15.data_ref, f32[3,3,32]{2,1,0:T(4,128)S(1)} %copy-done.4, f32[32]{0:T(128)S(1)} %copy-done.5, bf16[256,512]{1,0:T(8,128)(2,1)S(1)} %copy-done.1, bf16[256,512]{1,0:T(8,128)(2,1)S(1)} %copy-done, bf16[192,256]{1,0:T(8,128)(2,1)S(1)} %copy-done.2, ...), custom_call_target="tpu_custom_call" | custom-call | tf_op jit(solution)/shard_map/pallas_call | solution.py:279
  39.2 19.9 %all_to_all.16 = f32[64,1,640]{2,1,0:T(1,128)S(1)} all-to-all(f32[64,1,640]{2,1,0:T(1,128)S(1)} %bitcast.5), channel_id=1, replica_groups=mesh['seq'=64,'chan'=8] {'seq'}, dimensions={0} | all-to-all | bytes 327680 | tf_op jit(solution)/shard_map/all_to_all | solution.py:287
  59.1 10.0 %all_to_all.17.partial_ref = f32[8,8,128]{2,1,0:T(8,128)S(1)} all-to-all(f32[8,8,128]{2,1,0:T(8,128)S(1)} %shard_map.122), channel_id=1, replica_groups=mesh['seq'=64,'chan'=8] {'chan'}, dimensions={0} | all-to-all | bytes 65536 | tf_op jit(solution)/shard_map/all_to_all | solution.py:297
  69.1 0.7 shard_map.123
  (1 shorter events, 0.0 us)
Async XLA Ops:
  0.6 35.6 %copy-start.1 = (bf16[256,512]{1,0:T(8,128)(2,1)S(1)}, bf16[256,512]{1,0:T(8,128)(2,1)}, u32[]{:S(2)}) copy-start(bf16[256,512]{1,0:T(8,128)(2,1)} %constant.8.clone.high_ref) | copy-start | bytes 786436
  0.6 35.6 %copy-start.4 = (f32[3,3,32]{2,1,0:T(4,128)S(1)}, f32[3,3,32]{2,1,0:T(4,128)}, u32[]{:S(2)}) copy-start(f32[3,3,32]{2,1,0:T(4,128)} %taps_ref.1) | copy-start | bytes 3460
  0.7 35.6 %copy-start.5 = (f32[32]{0:T(128)S(1)}, f32[32]{0:T(128)}, u32[]{:S(2)}) copy-start(f32[32]{0:T(128)} %skip_ref.1) | copy-start | bytes 388
  2.5 33.7 %copy-start = (bf16[256,512]{1,0:T(8,128)(2,1)S(1)}, bf16[256,512]{1,0:T(8,128)(2,1)}, u32[]{:S(2)}) copy-start(bf16[256,512]{1,0:T(8,128)(2,1)} %constant.9.clone.low_ref) | copy-start | bytes 786436
  2.5 33.7 %copy-start.2 = (bf16[192,256]{1,0:T(8,128)(2,1)S(1)}, bf16[192,256]{1,0:T(8,128)(2,1)}, u32[]{:S(2)}) copy-start(bf16[192,256]{1,0:T(8,128)(2,1)} %constant.10.clone.strip_ref) | copy-start | bytes 294916
  2.5 33.7 %copy-start.3 = (f32[32,256]{1,0:T(8,128)S(1)}, f32[32,256]{1,0:T(8,128)}, u32[]{:S(2)}) copy-start(f32[32,256]{1,0:T(8,128)} %constant.11.clone.turn_ref) | copy-start | bytes 98308

commit v4 on v3

--- a/solution.py
+++ b/solution.py
@@ -16,7 +16,9 @@
 FILTERS = 32
 GROUPS = 8
 TAPS = 3
-ROWS = 5
+ROWS = 9
+RUN = 8
+PARTNERS = [[16 * a + RUN * b + z for a in range(4) for z in range(RUN)] for b in range(2)]
 TOTAL = BLOCKS * SPAN
 
 
@@ -109,8 +111,9 @@
         for side in range(2):
             piece = part[:, side * HALF : (side + 1) * HALF]
             row, tile = place_of(2 * i + side)
-            for copy in range(2):
-                rows_ref[copy * FILTERS : (copy + 1) * FILTERS, row, tile] = piece
+            for first in range(0, BLOCKS, RUN):
+                channel = first // (2 * RUN) * RUN
+                rows_ref[first : first + RUN, row, tile] = piece[channel : channel + RUN]
     out_ref[...] = rows_ref[...].astype(bf16)
 
 
@@ -132,7 +135,7 @@
     data_ref, taps_ref, skip_ref, high_ref, low_ref, strip_ref, turn_ref, out_ref, rows_ref
 ):
     place = lax.axis_index("seq")
-    channel = lax.rem(place, FILTERS)
+    channel = place // (2 * RUN) * RUN + lax.rem(place, RUN)
     rows_ref[...] = data_ref[...].astype(f32)
 
     def part(i):
@@ -202,29 +205,37 @@
     corr = result[:, 2 * SPAN :]
 
     grads = [grad * conv_out, dz * value, dz * key]
-    side = place // FILTERS
-
-    def mine(x):
-        return jnp.where(side == 0, x[:, :HALF], x[:, HALF:])
+    odd = lax.rem(place // RUN, 2)
+
+    def give(x, row):
+        runs = [
+            jnp.where(odd == 0, x[first : first + RUN], x[first + RUN : first + 2 * RUN])
+            for first in range(0, BLOCKS, 2 * RUN)
+        ]
+        mine = jnp.concatenate(runs, axis=0)
+        for side in range(2):
+            out_ref[pl.ds(row + side, FILTERS, stride=ROWS), :] = mine[
+                :, side * HALF : (side + 1) * HALF
+            ]
 
     for b in range(3):
         g = grads[b]
-        total = taps[b][0] * g + taps[b][1] * sooner(g, 1) + taps[b][2] * sooner(g, 2)
-        out_ref[pl.ds(b, BLOCKS, stride=ROWS), :] = mine(total)
-    out_ref[pl.ds(3, BLOCKS, stride=ROWS), :] = mine(corr)
+        give(taps[b][0] * g + taps[b][1] * sooner(g, 1) + taps[b][2] * sooner(g, 2), 2 * b)
+    give(corr, 6)
     sums = [whole_sum(grads[b] * moved[b][j]) for b in range(3) for j in range(TAPS)]
     sums.append(whole_sum(dw * product))
     lanes = lax.broadcasted_iota(jnp.int32, (1, HALF), 1)
     line = jnp.zeros((1, HALF), f32)
     for i, value in enumerate(sums):
         line = jnp.where(lanes == i, value, line)
-    out_ref[pl.ds(4, BLOCKS, stride=ROWS), :] = jnp.broadcast_to(line * TOTAL**-0.5, (BLOCKS, HALF))
+    line = jnp.broadcast_to(line * TOTAL**-0.5, (FILTERS, HALF))
+    out_ref[pl.ds(8, FILTERS, stride=ROWS), :] = line
 
 
 def filter_kernel(data_ref, out_ref):
     for group in range(GROUPS):
         for side in range(2):
-            first = ROWS * (FILTERS * side + 4 * group) + 3
+            first = ROWS * 4 * group + 6 + side
             out_ref[group, 4 * side : 4 * side + 4, :] = data_ref[pl.ds(first, 4, stride=ROWS), :]
 
 
@@ -232,9 +243,9 @@
     for b in range(3):
         for side in range(2):
             grads_ref[b, :, side * HALF : (side + 1) * HALF] = data_ref[
-                pl.ds(ROWS * FILTERS * side + b, FILTERS, stride=ROWS), :
+                pl.ds(2 * b + side, FILTERS, stride=ROWS), :
             ]
-    sums = data_ref[pl.ds(4, FILTERS, stride=ROWS), :]
+    sums = data_ref[pl.ds(8, FILTERS, stride=ROWS), :]
     padded = jnp.concatenate([sums, jnp.zeros((HALF - FILTERS, HALF), f32)], axis=0)
     flipped = padded.T[:, :FILTERS]
     for b in range(3):
@@ -278,15 +289,20 @@
     data = lax.all_to_all(message, "seq", split_axis=0, concat_axis=0, tiled=True)
     answer = pl.pallas_call(
         channel_kernel,
-        out_shape=like((BLOCKS * ROWS, HALF)),
+        out_shape=like((FILTERS * ROWS, HALF)),
         in_specs=[vmem, smem, smem] + [vmem] * 4,
         out_specs=vmem,
         scratch_shapes=[pltpu.VMEM((BLOCKS, 4, 3 * HALF), f32)],
         compiler_params=params,
     )(data, short_weights, skip, f_high, f_low, strip, turn)
     answer = lax.all_to_all(
-        answer.reshape(BLOCKS, 1, ROWS * HALF), "seq", split_axis=0, concat_axis=0, tiled=True
-    ).reshape(BLOCKS * ROWS, HALF)
+        answer.reshape(FILTERS, 1, ROWS * HALF),
+        "seq",
+        split_axis=0,
+        concat_axis=0,
+        tiled=True,
+        axis_index_groups=PARTNERS,
+    ).reshape(FILTERS * ROWS, HALF)
     partial = pl.pallas_call(
         filter_kernel,
         out_shape=like((GROUPS, 8, HALF)),

time: 70 us -> 64.4 us (0.920)
  blocking collectives: 63.6 us -> 58 us
    all_to_all x1, blocking collectives: 19.9 us -> 12.2 us  [body(): lax.all_to_all(answer.reshape(FILTERS, 1, ROWS * HALF), 'seq', split_axis...]
    all_to_all x1, blocking collectives: 10 us -> 12.2 us  [body(): lax.all_to_all(partial, 'chan', split_axis=0, concat_axis=0, tiled=True)]
where the time goes in v4:
time: 64.4 us; the launch traced here: 64.2 us
  blocking collectives  58 us (90%)
  Pallas kernels  5.41 us (8%)
  between operations  0.72 us (1%)
    all_to_all x1, blocking collectives, body(): lax.all_to_all(message, 'seq', split_axis=0, concat_axis=0, tiled=True)  33.7 us
    all_to_all x1, blocking collectives, body(): lax.all_to_all(answer.reshape(FILTERS, 1, ROWS * HALF), 'seq', split_axis...  12.2 us
    all_to_all x1, blocking collectives, body(): lax.all_to_all(partial, 'chan', split_axis=0, concat_axis=0, tiled=True)  12.2 us
    pallas_call x1, Pallas kernels, body(): pl.pallas_call(channel_kernel, out_shape=like((FILTERS * ROWS, HALF)), in...  2.91 us
    pallas_call x1, Pallas kernels, body(): pl.pallas_call(pack_kernel, out_shape=like((BLOCKS, 4, 3 * HALF), bf16),...  1.81 us

profile of v4, /device:TPU:1, one launch (start us, length us, event | category | flops | bytes accessed | tf_op | source)
XLA Modules:
  0.0 64.2 jit_solution(11295037265991978853)
XLA Ops:
  0.6 0.0 copy-start.1
  0.6 0.0 copy-start.4
  0.7 0.0 copy-start.5
  0.7 1.8 %shard_map.120 = bf16[64,4,384]{2,1,0:T(4,128)(2,1)} custom-call(bf16[3,32,256]{2,1,0:T(8,128)(2,1)} %inputs_hbm.1, bf16[32,256]{1,0:T(8,128)(2,1)} %grad_hbm.1, f32[32,256]{1,0:T(8,128)} %filters_hbm.1), custom_call_target="tpu_custom_call" | custom-call | tf_op jit(solution)/shard_map/pallas_call | solution.py:275
  2.5 0.0 copy-start
  2.5 0.0 copy-start.2
  2.5 0.0 copy-start.3
  2.5 33.7 %all_to_all.15.data_ref = bf16[64,4,384]{2,1,0:T(4,128)(2,1)S(1)} all-to-all(bf16[64,4,384]{2,1,0:T(4,128)(2,1)} %shard_map.120), channel_id=1, replica_groups=mesh['seq'=64,'chan'=8] {'seq'}, dimensions={0} | all-to-all | bytes 393216 | tf_op jit(solution)/shard_map/all_to_all | solution.py:289
  36.2 0.0 copy-done.1
  36.2 0.0 copy-done.4
  36.2 0.0 copy-done.5
  36.2 0.0 copy-done
  36.2 0.0 copy-done.2
  36.2 0.0 copy-done.3
  36.2 2.9 %shard_map.121 = f32[288,128]{1,0:T(8,128)S(1)} custom-call(bf16[64,4,384]{2,1,0:T(4,128)(2,1)S(1)} %all_to_all.15.data_ref, f32[3,3,32]{2,1,0:T(4,128)S(1)} %copy-done.4, f32[32]{0:T(128)S(1)} %copy-done.5, bf16[256,512]{1,0:T(8,128)(2,1)S(1)} %copy-done.1, bf16[256,512]{1,0:T(8,128)(2,1)S(1)} %copy-done, bf16[192,256]{1,0:T(8,128)(2,1)S(1)} %copy-done.2, ...), custom_call_target="tpu_custom_call" | custom-call | tf_op jit(solution)/shard_map/pallas_call | solution.py:290
  39.2 12.2 %all_to_all.16 = f32[32,1,1152]{2,1,0:T(1,128)S(1)} all-to-all(f32[32,1,1152]{2,1,0:T(1,128)S(1)} %bitcast.5), channel_id=1, replica_groups={{0,8,16,24,32,40,48,56,128,136,144,152,160,168,176,184,256,264,272,280,..., dimensions={0} | all-to-all | bytes 294912 | tf_op jit(solution)/shard_map/all_to_all | solution.py:298
  51.4 12.2 %all_to_all.17.partial_ref = f32[8,8,128]{2,1,0:T(8,128)S(1)} all-to-all(f32[8,8,128]{2,1,0:T(8,128)S(1)} %shard_map.122), channel_id=1, replica_groups=mesh['seq'=64,'chan'=8] {'chan'}, dimensions={0} | all-to-all | bytes 65536 | tf_op jit(solution)/shard_map/all_to_all | solution.py:313
  63.5 0.7 %shard_map.123 = (f32[3,32,256]{2,1,0:T(8,128)}, f32[1,32]{1,0:T(1,128)}, f32[3,3,32]{2,1,0:T(4,128)}, f32[4,256]{1,0:T(4,128)}) custom-call(f32[288,128]{1,0:T(8,128)S(1)} %bitcast.4, f32[8,8,128]{2,1,0:T(8,128)S(1)} %all_to_all.17.partial_ref), custom_call_target="tpu_custom_call" | custom-call | tf_op jit(solution)/shard_map/pallas_call | solution.py:314
  (1 shorter events, 0.0 us)
Async XLA Ops:
  0.6 35.6 %copy-start.1 = (bf16[256,512]{1,0:T(8,128)(2,1)S(1)}, bf16[256,512]{1,0:T(8,128)(2,1)}, u32[]{:S(2)}) copy-start(bf16[256,512]{1,0:T(8,128)(2,1)} %constant.8.clone.high_ref) | copy-start | bytes 786436
  0.6 35.6 %copy-start.4 = (f32[3,3,32]{2,1,0:T(4,128)S(1)}, f32[3,3,32]{2,1,0:T(4,128)}, u32[]{:S(2)}) copy-start(f32[3,3,32]{2,1,0:T(4,128)} %taps_ref.1) | copy-start | bytes 3460
  0.7 35.6 %copy-start.5 = (f32[32]{0:T(128)S(1)}, f32[32]{0:T(128)}, u32[]{:S(2)}) copy-start(f32[32]{0:T(128)} %skip_ref.1) | copy-start | bytes 388
  2.5 33.7 %copy-start = (bf16[256,512]{1,0:T(8,128)(2,1)S(1)}, bf16[256,512]{1,0:T(8,128)(2,1)}, u32[]{:S(2)}) copy-start(bf16[256,512]{1,0:T(8,128)(2,1)} %constant.9.clone.low_ref) | copy-start | bytes 786436
  2.5 33.7 %copy-start.2 = (bf16[192,256]{1,0:T(8,128)(2,1)S(1)}, bf16[192,256]{1,0:T(8,128)(2,1)}, u32[]{:S(2)}) copy-start(bf16[192,256]{1,0:T(8,128)(2,1)} %constant.10.clone.strip_ref) | copy-start | bytes 294916
  2.5 33.7 %copy-start.3 = (f32[32,256]{1,0:T(8,128)S(1)}, f32[32,256]{1,0:T(8,128)}, u32[]{:S(2)}) copy-start(f32[32,256]{1,0:T(8,128)} %constant.11.clone.turn_ref) | copy-start | bytes 98308

commit v5 on v4

--- a/solution.py
+++ b/solution.py
@@ -39,18 +39,22 @@
     t = g.T / TOTAL
     t_high, t_low = split_table(t)
     inverse_rows = np.concatenate([t_high, t_low], axis=1)
-    inner = 2 * math.pi * (cols[:, None] * cols[None, :] % SPAN) / SPAN
+    near = np.arange(HALF)
+    inner = 2 * math.pi * (near[:, None] * near[None, :] % HALF) / HALF
     f = np.concatenate([np.cos(inner), np.sin(inner)], axis=1)
     f_high, f_low = split_table(f)
+    points = np.concatenate([f_high, f_high, f_low], axis=0)
     strip = np.zeros((3 * BLOCKS, SPAN), dtype=jnp.bfloat16)
     strip[: 2 * BLOCKS, : 3 * BLOCKS] = forward_rows
     strip[2 * BLOCKS :] = inverse_rows
     eight = np.arange(8)
     coarse = 2 * math.pi * (32 * eight[:, None] * cols[None, :]) / (4.0 * TOTAL)
     fine = 2 * math.pi * ((4 * eight + 1)[:, None] * cols[None, :]) / (4.0 * TOTAL)
-    turn = np.concatenate([np.cos(coarse), np.sin(coarse), np.cos(fine), np.sin(fine)])
+    step = 2 * math.pi * near / SPAN
+    step = np.concatenate([np.cos(step), np.sin(step)])[None, :] * np.ones((8, 1))
+    turn = np.concatenate([np.cos(coarse), np.sin(coarse), np.cos(fine), np.sin(fine), step])
     turn = turn.astype(np.float32)
-    return f_high, f_low, strip, turn
+    return points, strip, turn
 
 
 def halves(x):
@@ -71,9 +75,9 @@
     return dot(table, jnp.concatenate([high, low, high], axis=0))
 
 
-def dot_right(x, f_high, f_low):
+def dot_right(x, table):
     high, low = halves(x)
-    return dot(high, f_high) + dot(low, f_high) + dot(high, f_low)
+    return dot(jnp.concatenate([high, low, high], axis=1), table)
 
 
 def later(x, n):
@@ -132,7 +136,7 @@
 
 
 def channel_kernel(
-    data_ref, taps_ref, skip_ref, high_ref, low_ref, strip_ref, turn_ref, out_ref, rows_ref
+    data_ref, taps_ref, skip_ref, points_ref, strip_ref, turn_ref, out_ref, rows_ref
 ):
     place = lax.axis_index("seq")
     channel = place // (2 * RUN) * RUN + lax.rem(place, RUN)
@@ -159,7 +163,8 @@
     dw = grad * query
 
     cosine, sine = turns(turn_ref)
-    f_high, f_low = high_ref[...], low_ref[...]
+    points = points_ref[...]
+    odd_cos, odd_sin = turn_ref[32:33, :HALF], turn_ref[32:33, HALF:]
     left = strip_ref[: 2 * BLOCKS, : 3 * BLOCKS]
     right = strip_ref[2 * BLOCKS :, :]
     right = jnp.concatenate([right[:, :HALF], right], axis=1)
@@ -168,34 +173,43 @@
     for i in range(3):
         re = start[:BLOCKS, i * SPAN : (i + 1) * SPAN]
         im = start[BLOCKS:, i * SPAN : (i + 1) * SPAN]
-        stacked.append(re * cosine + im * sine)
-        stacked.append(im * cosine - re * sine)
-    spec = dot_right(jnp.concatenate(stacked, axis=0), f_high, f_low)
+        re, im = re * cosine + im * sine, im * cosine - re * sine
+        stacked += [re[:, :HALF] + re[:, HALF:], im[:, :HALF] + im[:, HALF:]]
+        re, im = re[:, :HALF] - re[:, HALF:], im[:, :HALF] - im[:, HALF:]
+        stacked += [re * odd_cos + im * odd_sin, im * odd_cos - re * odd_sin]
+    spec = dot_right(jnp.concatenate(stacked, axis=0), points)
+
+    def pair(values, i):
+        re = values[2 * i * BLOCKS : (2 * i + 1) * BLOCKS]
+        im = values[(2 * i + 1) * BLOCKS : (2 * i + 2) * BLOCKS]
+        return re[:, :HALF], re[:, HALF:], im[:, :HALF], im[:, HALF:]
 
     def spectrum(i):
-        re = spec[2 * i * BLOCKS : (2 * i + 1) * BLOCKS]
-        im = spec[(2 * i + 1) * BLOCKS : (2 * i + 2) * BLOCKS]
-        return re[:, :SPAN] + im[:, SPAN:], im[:, :SPAN] - re[:, SPAN:]
+        res, ims = [], []
+        for part in (2 * i, 2 * i + 1):
+            re_cos, re_sin, im_cos, im_sin = pair(spec, part)
+            res.append(re_cos + im_sin)
+            ims.append(im_cos - re_sin)
+        return res, ims
 
     (p_re, p_im), (d_re, d_im), (h_re, h_im) = [spectrum(i) for i in range(3)]
-    joined = jnp.concatenate(
-        [
-            h_re * p_re - h_im * p_im,
-            h_re * p_im + h_im * p_re,
-            d_re * h_re + d_im * h_im,
-            d_im * h_re - d_re * h_im,
-            d_re * p_re + d_im * p_im,
-            d_im * p_re - d_re * p_im,
-        ],
-        axis=0,
-    )
-    back = dot_right(joined, f_high, f_low)
+    joined = []
+    for e in range(2):
+        joined += [h_re[e] * p_re[e] - h_im[e] * p_im[e], h_re[e] * p_im[e] + h_im[e] * p_re[e]]
+    for e in range(2):
+        joined += [d_re[e] * h_re[e] + d_im[e] * h_im[e], d_im[e] * h_re[e] - d_re[e] * h_im[e]]
+    for e in range(2):
+        joined += [d_re[e] * p_re[e] + d_im[e] * p_im[e], d_im[e] * p_re[e] - d_re[e] * p_im[e]]
+    back = dot_right(jnp.concatenate(joined, axis=0), points)
     turned = []
     for i in range(3):
-        re = back[2 * i * BLOCKS : (2 * i + 1) * BLOCKS]
-        im = back[(2 * i + 1) * BLOCKS : (2 * i + 2) * BLOCKS]
-        b_re = re[:, :SPAN] - im[:, SPAN:]
-        b_im = im[:, :SPAN] + re[:, SPAN:]
+        re_cos, re_sin, im_cos, im_sin = pair(back, 2 * i)
+        even_re, even_im = re_cos - im_sin, im_cos + re_sin
+        re_cos, re_sin, im_cos, im_sin = pair(back, 2 * i + 1)
+        re, im = re_cos - im_sin, im_cos + re_sin
+        re, im = re * odd_cos - im * odd_sin, im * odd_cos + re * odd_sin
+        b_re = jnp.concatenate([even_re + re, even_re - re], axis=1)
+        b_im = jnp.concatenate([even_im + im, even_im - im], axis=1)
         turned.append(
             jnp.concatenate([b_re * cosine - b_im * sine, b_im * cosine + b_re * sine], axis=0)
         )
@@ -271,7 +285,7 @@
 
 
 def body(inputs, short_weights, filters, skip, grad_out):
-    f_high, f_low, strip, turn = [jnp.asarray(values) for values in tables()]
+    points, strip, turn = [jnp.asarray(values) for values in tables()]
     message = pl.pallas_call(
         pack_kernel,
         out_shape=like((BLOCKS, 4, 3 * HALF), bf16),
@@ -290,11 +304,11 @@
     answer = pl.pallas_call(
         channel_kernel,
         out_shape=like((FILTERS * ROWS, HALF)),
-        in_specs=[vmem, smem, smem] + [vmem] * 4,
+        in_specs=[vmem, smem, smem] + [vmem] * 3,
         out_specs=vmem,
         scratch_shapes=[pltpu.VMEM((BLOCKS, 4, 3 * HALF), f32)],
         compiler_params=params,
-    )(data, short_weights, skip, f_high, f_low, strip, turn)
+    )(data, short_weights, skip, points, strip, turn)
     answer = lax.all_to_all(
         answer.reshape(FILTERS, 1, ROWS * HALF),
         "seq",

time: 64.4 us -> 63.9 us (level)
  no operation moved by 1% of the time
where the time goes in v5:
time: 63.9 us; the launch traced here: 63.6 us
  blocking collectives  58 us (91%)
  Pallas kernels  4.82 us (8%)
  between operations  0.7 us (1%)
    all_to_all x1, blocking collectives, body(): lax.all_to_all(message, 'seq', split_axis=0, concat_axis=0, tiled=True)  33.7 us
    all_to_all x1, blocking collectives, body(): lax.all_to_all(answer.reshape(FILTERS, 1, ROWS * HALF), 'seq', split_axis...  12.2 us
    all_to_all x1, blocking collectives, body(): lax.all_to_all(partial, 'chan', split_axis=0, concat_axis=0, tiled=True)  12.2 us
    pallas_call x1, Pallas kernels, body(): pl.pallas_call(channel_kernel, out_shape=like((FILTERS * ROWS, HALF)), in...  2.36 us
    pallas_call x1, Pallas kernels, body(): pl.pallas_call(pack_kernel, out_shape=like((BLOCKS, 4, 3 * HALF), bf16),...  1.78 us

profile of v5, /device:TPU:1, one launch (start us, length us, event | category | flops | bytes accessed | tf_op | source)
XLA Modules:
  0.0 63.6 jit_solution(17875840769454344896)
XLA Ops:
  0.6 1.8 %shard_map.111 = bf16[64,4,384]{2,1,0:T(4,128)(2,1)} custom-call(bf16[3,32,256]{2,1,0:T(8,128)(2,1)} %inputs_hbm.1, bf16[32,256]{1,0:T(8,128)(2,1)} %grad_hbm.1, f32[32,256]{1,0:T(8,128)} %filters_hbm.1), custom_call_target="tpu_custom_call" | custom-call | tf_op jit(solution)/shard_map/pallas_call | solution.py:289
  2.4 0.0 copy-start
  2.4 0.0 copy-start.1
  2.4 0.0 copy-start.2
  2.5 0.0 copy-start.3
  2.5 0.0 copy-start.4
  2.5 33.7 %all_to_all.15.data_ref = bf16[64,4,384]{2,1,0:T(4,128)(2,1)S(1)} all-to-all(bf16[64,4,384]{2,1,0:T(4,128)(2,1)} %shard_map.111), channel_id=1, replica_groups=mesh['seq'=64,'chan'=8] {'seq'}, dimensions={0} | all-to-all | bytes 393216 | tf_op jit(solution)/shard_map/all_to_all | solution.py:303
  36.2 0.0 copy-done
  36.2 0.0 copy-done.1
  36.2 0.0 copy-done.2
  36.2 0.0 copy-done.3
  36.2 0.0 copy-done.4
  36.2 2.4 %shard_map.112 = f32[288,128]{1,0:T(8,128)S(1)} custom-call(bf16[64,4,384]{2,1,0:T(4,128)(2,1)S(1)} %all_to_all.15.data_ref, f32[3,3,32]{2,1,0:T(4,128)S(1)} %copy-done.3, f32[32]{0:T(128)S(1)} %copy-done.4, bf16[384,256]{1,0:T(8,128)(2,1)S(1)} %copy-done, bf16[192,256]{1,0:T(8,128)(2,1)S(1)} %copy-done.1, f32[40,256]{1,0:T(8,128)S(1)} %copy-done.2), custom_call_target="tpu_custom_call" | custom-call | tf_op jit(solution)/shard_map/pallas_call | solution.py:304
  38.6 12.2 %all_to_all.16 = f32[32,1,1152]{2,1,0:T(1,128)S(1)} all-to-all(f32[32,1,1152]{2,1,0:T(1,128)S(1)} %bitcast.5), channel_id=1, replica_groups={{0,8,16,24,32,40,48,56,128,136,144,152,160,168,176,184,256,264,272,280,..., dimensions={0} | all-to-all | bytes 294912 | tf_op jit(solution)/shard_map/all_to_all | solution.py:312
  50.7 12.2 %all_to_all.17.partial_ref = f32[8,8,128]{2,1,0:T(8,128)S(1)} all-to-all(f32[8,8,128]{2,1,0:T(8,128)S(1)} %shard_map.113), channel_id=1, replica_groups=mesh['seq'=64,'chan'=8] {'chan'}, dimensions={0} | all-to-all | bytes 65536 | tf_op jit(solution)/shard_map/all_to_all | solution.py:327
  62.9 0.7 %shard_map.114 = (f32[3,32,256]{2,1,0:T(8,128)}, f32[1,32]{1,0:T(1,128)}, f32[3,3,32]{2,1,0:T(4,128)}, f32[4,256]{1,0:T(4,128)}) custom-call(f32[288,128]{1,0:T(8,128)S(1)} %bitcast.4, f32[8,8,128]{2,1,0:T(8,128)S(1)} %all_to_all.17.partial_ref), custom_call_target="tpu_custom_call" | custom-call | tf_op jit(solution)/shard_map/pallas_call | solution.py:328
  (1 shorter events, 0.0 us)
Async XLA Ops:
  2.4 33.7 %copy-start = (bf16[384,256]{1,0:T(8,128)(2,1)S(1)}, bf16[384,256]{1,0:T(8,128)(2,1)}, u32[]{:S(2)}) copy-start(bf16[384,256]{1,0:T(8,128)(2,1)} %constant.6.clone.points_ref) | copy-start | bytes 589828
  2.4 33.7 %copy-start.1 = (bf16[192,256]{1,0:T(8,128)(2,1)S(1)}, bf16[192,256]{1,0:T(8,128)(2,1)}, u32[]{:S(2)}) copy-start(bf16[192,256]{1,0:T(8,128)(2,1)} %constant.7.clone.strip_ref) | copy-start | bytes 294916
  2.4 33.7 %copy-start.2 = (f32[40,256]{1,0:T(8,128)S(1)}, f32[40,256]{1,0:T(8,128)}, u32[]{:S(2)}) copy-start(f32[40,256]{1,0:T(8,128)} %constant.8.clone.turn_ref) | copy-start | bytes 122884
  2.5 33.7 %copy-start.3 = (f32[3,3,32]{2,1,0:T(4,128)S(1)}, f32[3,3,32]{2,1,0:T(4,128)}, u32[]{:S(2)}) copy-start(f32[3,3,32]{2,1,0:T(4,128)} %taps_ref.1) | copy-start | bytes 3460
  2.5 33.7 %copy-start.4 = (f32[32]{0:T(128)S(1)}, f32[32]{0:T(128)}, u32[]{:S(2)}) copy-start(f32[32]{0:T(128)} %skip_ref.1) | copy-start | bytes 388

commit v6 on v5

--- a/solution.py
+++ b/solution.py
@@ -277,7 +277,6 @@
 hbm = pl.BlockSpec(memory_space=pltpu.HBM)
 smem = pl.BlockSpec(memory_space=pltpu.SMEM)
 params = pltpu.CompilerParams(vmem_limit_bytes=32 * 1024 * 1024)
-pack_params = pltpu.CompilerParams(vmem_limit_bytes=56 * 1024 * 1024)
 
 
 def like(shape, dtype=f32):
@@ -298,8 +297,8 @@
             pltpu.VMEM((BLOCKS, 4, 3 * HALF), f32),
             pltpu.SemaphoreType.DMA((3,)),
         ],
-        compiler_params=pack_params,
-    )(inputs, grad_out, filters)
+        compiler_params=params,
+    )(*[pltpu.with_memory_space_constraint(x, pltpu.HBM) for x in (inputs, grad_out, filters)])
     data = lax.all_to_all(message, "seq", split_axis=0, concat_axis=0, tiled=True)
     answer = pl.pallas_call(
         channel_kernel,

time: 63.9 us -> 63 us (0.986)
  Pallas kernels: 4.82 us -> 4.16 us
    pallas_call x1, Pallas kernels: 1.78 us -> 1.11 us  [body(): pl.pallas_call(pack_kernel, out_shape=like((BLOCKS, 4, 3 * HALF), bf16),...]
where the time goes in v6:
time: 63 us; the launch traced here: 62.7 us
  blocking collectives  57.8 us (92%)
  Pallas kernels  4.16 us (7%)
  between operations  0.7 us (1%)
    all_to_all x1, blocking collectives, body(): lax.all_to_all(message, 'seq', split_axis=0, concat_axis=0, tiled=True)  33.5 us
    all_to_all x1, blocking collectives, body(): lax.all_to_all(answer.reshape(FILTERS, 1, ROWS * HALF), 'seq', split_axis...  12.2 us
    all_to_all x1, blocking collectives, body(): lax.all_to_all(partial, 'chan', split_axis=0, concat_axis=0, tiled=True)  12.2 us
    pallas_call x1, Pallas kernels, body(): pl.pallas_call(channel_kernel, out_shape=like((FILTERS * ROWS, HALF)), in...  2.37 us

profile of v6, /device:TPU:1, one launch (start us, length us, event | category | flops | bytes accessed | tf_op | source)
XLA Modules:
  0.0 62.7 jit_solution(5934006318124281942)
XLA Ops:
  0.6 1.1 %shard_map.111 = bf16[64,4,384]{2,1,0:T(4,128)(2,1)S(1)} custom-call(bf16[3,32,256]{2,1,0:T(8,128)(2,1)} %inputs_hbm.1, bf16[32,256]{1,0:T(8,128)(2,1)} %grad_hbm.1, f32[32,256]{1,0:T(8,128)} %filters_hbm.1), custom_call_target="tpu_custom_call" | custom-call | tf_op jit(solution)/shard_map/pallas_call | solution.py:288
  1.8 0.0 copy-start
  1.8 0.0 copy-start.1
  1.8 0.0 copy-start.2
  1.8 0.0 copy-start.3
  1.8 0.0 copy-start.4
  1.8 33.5 %all_to_all.15.data_ref = bf16[64,4,384]{2,1,0:T(4,128)(2,1)S(1)} all-to-all(bf16[64,4,384]{2,1,0:T(4,128)(2,1)S(1)} %shard_map.111), channel_id=1, replica_groups=mesh['seq'=64,'chan'=8] {'seq'}, dimensions={0} | all-to-all | bytes 393216 | tf_op jit(solution)/shard_map/all_to_all | solution.py:302
  35.3 0.0 copy-done
  35.3 0.0 copy-done.1
  35.3 0.0 copy-done.2
  35.3 0.0 copy-done.3
  35.3 0.0 copy-done.4
  35.3 2.4 %shard_map.112 = f32[288,128]{1,0:T(8,128)S(1)} custom-call(bf16[64,4,384]{2,1,0:T(4,128)(2,1)S(1)} %all_to_all.15.data_ref, f32[3,3,32]{2,1,0:T(4,128)S(1)} %copy-done.3, f32[32]{0:T(128)S(1)} %copy-done.4, bf16[384,256]{1,0:T(8,128)(2,1)S(1)} %copy-done, bf16[192,256]{1,0:T(8,128)(2,1)S(1)} %copy-done.1, f32[40,256]{1,0:T(8,128)S(1)} %copy-done.2), custom_call_target="tpu_custom_call" | custom-call | tf_op jit(solution)/shard_map/pallas_call | solution.py:303
  37.7 12.2 %all_to_all.16 = f32[32,1,1152]{2,1,0:T(1,128)S(1)} all-to-all(f32[32,1,1152]{2,1,0:T(1,128)S(1)} %bitcast.5), channel_id=1, replica_groups={{0,8,16,24,32,40,48,56,128,136,144,152,160,168,176,184,256,264,272,280,..., dimensions={0} | all-to-all | bytes 294912 | tf_op jit(solution)/shard_map/all_to_all | solution.py:311
  49.9 12.2 %all_to_all.17.partial_ref = f32[8,8,128]{2,1,0:T(8,128)S(1)} all-to-all(f32[8,8,128]{2,1,0:T(8,128)S(1)} %shard_map.113), channel_id=1, replica_groups=mesh['seq'=64,'chan'=8] {'chan'}, dimensions={0} | all-to-all | bytes 65536 | tf_op jit(solution)/shard_map/all_to_all | solution.py:326
  62.0 0.7 %shard_map.114 = (f32[3,32,256]{2,1,0:T(8,128)}, f32[1,32]{1,0:T(1,128)}, f32[3,3,32]{2,1,0:T(4,128)}, f32[4,256]{1,0:T(4,128)}) custom-call(f32[288,128]{1,0:T(8,128)S(1)} %bitcast.4, f32[8,8,128]{2,1,0:T(8,128)S(1)} %all_to_all.17.partial_ref), custom_call_target="tpu_custom_call" | custom-call | tf_op jit(solution)/shard_map/pallas_call | solution.py:327
  (1 shorter events, 0.0 us)
Async XLA Ops:
  1.8 33.5 %copy-start = (bf16[384,256]{1,0:T(8,128)(2,1)S(1)}, bf16[384,256]{1,0:T(8,128)(2,1)}, u32[]{:S(2)}) copy-start(bf16[384,256]{1,0:T(8,128)(2,1)} %constant.6.clone.points_ref) | copy-start | bytes 589828
  1.8 33.5 %copy-start.1 = (bf16[192,256]{1,0:T(8,128)(2,1)S(1)}, bf16[192,256]{1,0:T(8,128)(2,1)}, u32[]{:S(2)}) copy-start(bf16[192,256]{1,0:T(8,128)(2,1)} %constant.7.clone.strip_ref) | copy-start | bytes 294916
  1.8 33.5 %copy-start.2 = (f32[40,256]{1,0:T(8,128)S(1)}, f32[40,256]{1,0:T(8,128)}, u32[]{:S(2)}) copy-start(f32[40,256]{1,0:T(8,128)} %constant.8.clone.turn_ref) | copy-start | bytes 122884
  1.8 33.5 %copy-start.3 = (f32[3,3,32]{2,1,0:T(4,128)S(1)}, f32[3,3,32]{2,1,0:T(4,128)}, u32[]{:S(2)}) copy-start(f32[3,3,32]{2,1,0:T(4,128)} %taps_ref.1) | copy-start | bytes 3460
  1.8 33.5 %copy-start.4 = (f32[32]{0:T(128)S(1)}, f32[32]{0:T(128)}, u32[]{:S(2)}) copy-start(f32[32]{0:T(128)} %skip_ref.1) | copy-start | bytes 388

commit v7 on v6

v7 whole, which is shorter than its diff:
```python
import math

import jax
import jax.numpy as jnp
import numpy as np
from jax import lax
from jax.experimental import pallas as pl
from jax.experimental.pallas import tpu as pltpu
from jax.sharding import PartitionSpec as P

f32 = jnp.float32
bf16 = jnp.bfloat16
BLOCKS = 64
SPAN = 256
HALF = 128
FILTERS = 32
GROUPS = 8
TAPS = 3
ROWS = 9
RUN = 8
PARTNERS = [[16 * x + RUN * b + z for x in range(4) for z in range(RUN)] for b in range(2)]


TOTAL = BLOCKS * SPAN


def is_far(g, owner):
    return abs(g // 2 - owner // 2) == 3


def owner_route():
    route = []
    for place in range(BLOCKS):
        for g in range(GROUPS):
            owner = place % RUN ^ g
            target = place ^ RUN if is_far(g, owner) else place
            route.append((place * GROUPS + g, target * GROUPS + owner))
    return route


def split_table(values):
    high = values.astype(jnp.bfloat16)
    low = (values - high.astype(np.float64)).astype(jnp.bfloat16)
    return high, low


def tables():
    rows = np.arange(BLOCKS)
    cols = np.arange(SPAN)
    odd = 4 * rows + 1
    outer = 2 * math.pi * (odd[:, None] * rows[None, :] % 256) / 256.0
    g = np.concatenate([np.cos(outer), -np.sin(outer)], axis=0)
    g_high, g_low = split_table(g)
    forward_rows = np.concatenate([g_high, g_high, g_low], axis=1)
    t = g.T / TOTAL
    t_high, t_low = split_table(t)
    inverse_rows = np.concatenate([t_high, t_low], axis=1)
    near = np.arange(HALF)
    inner = 2 * math.pi * (near[:, None] * near[None, :] % HALF) / HALF
    f = np.concatenate([np.cos(inner), np.sin(inner)], axis=1)
    f_high, f_low = split_table(f)
    points = np.concatenate([f_high, f_high, f_low], axis=0)
    strip = np.zeros((3 * BLOCKS, SPAN), dtype=jnp.bfloat16)
    strip[: 2 * BLOCKS, : 3 * BLOCKS] = forward_rows
    strip[2 * BLOCKS :] = inverse_rows
    eight = np.arange(8)
    coarse = 2 * math.pi * (32 * eight[:, None] * cols[None, :]) / (4.0 * TOTAL)
    fine = 2 * math.pi * ((4 * eight + 1)[:, None] * cols[None, :]) / (4.0 * TOTAL)
    step = 2 * math.pi * near / SPAN
    step = np.concatenate([np.cos(step), np.sin(step)])[None, :] * np.ones((8, 1))
    turn = np.concatenate([np.cos(coarse), np.sin(coarse), np.cos(fine), np.sin(fine), step])
    turn = turn.astype(np.float32)
    return points, strip, turn


def halves(x):
    high = x.astype(bf16)
    return high, (x - high.astype(f32)).astype(bf16)


def place_of(i):
    return i % 4, slice(i // 4 * HALF, (i // 4 + 1) * HALF)


def dot(a, b):
    return jnp.dot(a, b, preferred_element_type=f32)


def dot_left(table, x):
    high, low = halves(x)
    return dot(table, jnp.concatenate([high, low, high], axis=0))


def dot_right(x, table):
    high, low = halves(x)
    return dot(jnp.concatenate([high, low, high], axis=1), table)


def later(x, n):
    row = lax.broadcasted_iota(jnp.int32, x.shape, 0)
    col = lax.broadcasted_iota(jnp.int32, x.shape, 1)
    here = pltpu.roll(x, n, 1)
    above = jnp.where(row == 0, 0.0, pltpu.roll(here, 1, 0))
    return jnp.where(col < n, above, here)


def sooner(x, n):
    row = lax.broadcasted_iota(jnp.int32, x.shape, 0)
    col = lax.broadcasted_iota(jnp.int32, x.shape, 1)
    here = pltpu.roll(x, SPAN - n, 1)
    below = jnp.where(row == BLOCKS - 1, 0.0, pltpu.roll(here, BLOCKS - 1, 0))
    return jnp.where(col >= SPAN - n, below, here)


def pack_kernel(inputs_hbm, grad_hbm, filters_hbm, out_ref, inputs_ref, grad_ref, filters_ref, rows_ref, short_ref, sems):
    copies = [
        pltpu.make_async_copy(source, target, sems.at[i])
        for i, (source, target) in enumerate(
            [(inputs_hbm, inputs_ref), (grad_hbm, grad_ref), (filters_hbm, filters_ref)]
        )
    ]
    for copy in copies:
        copy.start()
    for copy in copies:
        copy.wait()
    h = filters_ref[...]
    h_high = h.astype(bf16).astype(f32)
    parts = [inputs_ref[b].astype(f32) for b in range(3)]
    parts += [grad_ref[...].astype(f32), h_high, h - h_high]
    for i, part in enumerate(parts):
        for side in range(2):
            row, tile = place_of(2 * i + side)
            rows_ref[:, row, tile] = part[:, side * HALF : (side + 1) * HALF]
    short_ref[...] = rows_ref[...].astype(bf16)
    g = lax.axis_index("chan")
    for place in range(BLOCKS):
        out_ref[place] = short_ref[4 * jnp.bitwise_xor(g, place % RUN) + place // (2 * RUN)]


def whole_sum(x):
    return jnp.sum(jnp.sum(x, axis=0, keepdims=True), axis=1, keepdims=True)


def turns(turn_ref):
    cosines, sines = [], []
    fine_cos, fine_sin = turn_ref[16:24, :], turn_ref[24:32, :]
    for a in range(8):
        coarse_cos, coarse_sin = turn_ref[a : a + 1, :], turn_ref[8 + a : 9 + a, :]
        cosines.append(coarse_cos * fine_cos - coarse_sin * fine_sin)
        sines.append(coarse_sin * fine_cos + coarse_cos * fine_sin)
    return jnp.concatenate(cosines, axis=0), jnp.concatenate(sines, axis=0)


def seat():
    place, g = lax.axis_index("seq"), lax.axis_index("chan")
    owner = jnp.bitwise_xor(lax.rem(place, RUN), g)
    return g, owner, 4 * owner + place // (2 * RUN), lax.rem(place // RUN, 2)


def unpack(data_ref, rows_ref):
    rows_ref[...] = data_ref[...].astype(f32)
    parts = []
    for i in range(6):
        pieces = []
        for side in range(2):
            row, tile = place_of(2 * i + side)
            pieces.append(rows_ref[:, row, tile])
        parts.append(jnp.concatenate(pieces, axis=1))
    return parts


def mix(branch, taps):
    moved = [[x] + [later(x, j) for j in range(1, TAPS)] for x in branch]
    mixed = [
        taps[b][0] * moved[b][0] + taps[b][1] * moved[b][1] + taps[b][2] * moved[b][2]
        for b in range(3)
    ]
    return moved, mixed


def constants(strip_ref, turn_ref):
    left = strip_ref[: 2 * BLOCKS, : 3 * BLOCKS]
    right = strip_ref[2 * BLOCKS :, :]
    right = jnp.concatenate([right[:, :HALF], right], axis=1)
    odd = turn_ref[32:33, :HALF], turn_ref[32:33, HALF:]
    return left, right, turns(turn_ref), odd


def pair(values, i):
    re = values[2 * i * BLOCKS : (2 * i + 1) * BLOCKS]
    im = values[(2 * i + 1) * BLOCKS : (2 * i + 2) * BLOCKS]
    return re[:, :HALF], re[:, HALF:], im[:, :HALF], im[:, HALF:]


def spectra(signals, points, left, turn, odd):
    cosine, sine = turn
    odd_cos, odd_sin = odd
    start = dot_left(left, jnp.concatenate(signals, axis=1))
    stacked = []
    for i in range(len(signals)):
        re = start[:BLOCKS, i * SPAN : (i + 1) * SPAN]
        im = start[BLOCKS:, i * SPAN : (i + 1) * SPAN]
        re, im = re * cosine + im * sine, im * cosine - re * sine
        stacked += [re[:, :HALF] + re[:, HALF:], im[:, :HALF] + im[:, HALF:]]
        re, im = re[:, :HALF] - re[:, HALF:], im[:, :HALF] - im[:, HALF:]
        stacked += [re * odd_cos + im * odd_sin, im * odd_cos - re * odd_sin]
    values = dot_right(jnp.concatenate(stacked, axis=0), points)
    results = []
    for i in range(2 * len(signals)):
        re_cos, re_sin, im_cos, im_sin = pair(values, i)
        results.append((re_cos + im_sin, im_cos - re_sin))
    return [results[2 * i : 2 * i + 2] for i in range(len(signals))]


def times(a, b):
    return a[0] * b[0] - a[1] * b[1], a[0] * b[1] + a[1] * b[0]


def times_conj(a, b):
    return a[0] * b[0] + a[1] * b[1], a[1] * b[0] - a[0] * b[1]


def inverse(spectrums, points, right, turn, odd):
    cosine, sine = turn
    odd_cos, odd_sin = odd
    joined = [x for spectrum in spectrums for part in spectrum for x in part]
    back = dot_right(jnp.concatenate(joined, axis=0), points)
    turned = []
    for i in range(len(spectrums)):
        re_cos, re_sin, im_cos, im_sin = pair(back, 2 * i)
        even_re, even_im = re_cos - im_sin, im_cos + re_sin
        re_cos, re_sin, im_cos, im_sin = pair(back, 2 * i + 1)
        re, im = re_cos - im_sin, im_cos + re_sin
        re, im = re * odd_cos - im * odd_sin, im * odd_cos + re * odd_sin
        b_re = jnp.concatenate([even_re + re, even_re - re], axis=1)
        b_im = jnp.concatenate([even_im + im, even_im - im], axis=1)
        turned.append(
            jnp.concatenate([b_re * cosine - b_im * sine, b_im * cosine + b_re * sine], axis=0)
        )
    return dot_left(right, jnp.concatenate(turned, axis=1))


def every_second_run(x, b):
    runs = [
        jnp.where(b == 0, x[first : first + RUN], x[first + RUN : first + 2 * RUN])
        for first in range(0, BLOCKS, 2 * RUN)
    ]
    return jnp.concatenate(runs, axis=0)


def corr_kernel(
    data_ref, taps_ref, skip_ref, points_ref, strip_ref, turn_ref, corr_ref, spec_ref, rows_ref
):
    g, owner, channel, b_own = seat()
    parts = unpack(data_ref, rows_ref)
    taps = [[taps_ref[b, j, channel] for j in range(TAPS)] for b in range(3)]
    _, (query, key, value) = mix(parts[:3], taps)
    product, dw = key * value, parts[3] * query
    left, right, turn, odd = constants(strip_ref, turn_ref)
    points = points_ref[...]
    p, d = spectra([product, dw], points, left, turn, odd)
    for i, x in enumerate([x for spectrum in (p, d) for part in spectrum for x in part]):
        spec_ref[i * BLOCKS : (i + 1) * BLOCKS, :] = x
    corr = inverse([[times_conj(d[e], p[e]) for e in range(2)]], points, right, turn, odd)
    b_there = jnp.where(is_far(g, owner), 1 - b_own, b_own)
    corr = every_second_run(corr, b_there)
    for side in range(2):
        corr_ref[side * FILTERS : (side + 1) * FILTERS, :] = corr[:, side * HALF : (side + 1) * HALF]


def channel_kernel(
    data_ref, taps_ref, skip_ref, points_ref, strip_ref, turn_ref, spec_ref, out_ref, rows_ref
):
    _, _, channel, b_own = seat()
    parts = unpack(data_ref, rows_ref)
    grad, h = parts[3], parts[4] + parts[5]
    taps = [[taps_ref[b, j, channel] for j in range(TAPS)] for b in range(3)]
    direct = skip_ref[channel]
    moved, (query, key, value) = mix(parts[:3], taps)
    product, dw = key * value, grad * query
    left, right, turn, odd = constants(strip_ref, turn_ref)
    points = points_ref[...]
    (h_spec,) = spectra([h], points, left, turn, odd)
    held = [spec_ref[i * BLOCKS : (i + 1) * BLOCKS, :] for i in range(8)]
    p = [(held[0], held[1]), (held[2], held[3])]
    d = [(held[4], held[5]), (held[6], held[7])]
    result = inverse(
        [
            [times(h_spec[e], p[e]) for e in range(2)],
            [times_conj(d[e], h_spec[e]) for e in range(2)],
        ],
        points,
        right,
        turn,
        odd,
    )
    conv_out = result[:, :SPAN] + direct * product
    dz = result[:, SPAN:] + direct * dw

    grads = [grad * conv_out, dz * value, dz * key]
    for b in range(3):
        g = grads[b]
        total = taps[b][0] * g + taps[b][1] * sooner(g, 1) + taps[b][2] * sooner(g, 2)
        mine = every_second_run(total, b_own)
        for side in range(2):
            out_ref[pl.ds(2 * b + side, FILTERS, stride=ROWS), :] = mine[
                :, side * HALF : (side + 1) * HALF
            ]
    for row in (6, 7):
        out_ref[pl.ds(row, FILTERS, stride=ROWS), :] = jnp.zeros((FILTERS, HALF), f32)
    sums = [whole_sum(grads[b] * moved[b][j]) for b in range(3) for j in range(TAPS)]
    sums.append(whole_sum(dw * product))
    lanes = lax.broadcasted_iota(jnp.int32, (1, HALF), 1)
    line = jnp.zeros((1, HALF), f32)
    for i, value in enumerate(sums):
        line = jnp.where(lanes == i, value, line)
    line = jnp.broadcast_to(line * TOTAL**-0.5, (FILTERS, HALF))
    out_ref[pl.ds(8, FILTERS, stride=ROWS), :] = line


def merge_kernel(answer_ref, corr_ref, out_ref):
    out_ref[...] = answer_ref[...]
    for side in range(2):
        out_ref[pl.ds(6 + side, FILTERS, stride=ROWS), :] = corr_ref[
            side * FILTERS : (side + 1) * FILTERS, :
        ]


def place_kernel(data_ref, grads_ref, skip_ref, short_ref, filter_ref, sums_ref):
    g = lax.axis_index("chan")
    for owner in range(GROUPS):
        first = ROWS * jnp.bitwise_xor(g, owner)
        rows = slice(4 * owner, 4 * owner + 4)
        for b in range(3):
            for side in range(2):
                grads_ref[b, rows, side * HALF : (side + 1) * HALF] = data_ref[
                    pl.ds(first + (2 * b + side), 4, stride=RUN * ROWS), :
                ]
        sums_ref[rows, :] = data_ref[pl.ds(first + 8, 4, stride=RUN * ROWS), :]
    padded = jnp.concatenate([sums_ref[...], jnp.zeros((HALF - FILTERS, HALF), f32)], axis=0)
    flipped = padded.T[:, :FILTERS]
    for b in range(3):
        short_ref[b] = flipped[TAPS * b : TAPS * (b + 1), :]
    skip_ref[...] = flipped[9:10, :]
    for x in range(4):
        for side in range(2):
            terms = data_ref[pl.ds(x * RUN * ROWS + 6 + side, RUN, stride=ROWS), :]
            total = jnp.sum(terms, axis=0, keepdims=True) * (TOTAL * GROUPS) ** -0.5
            filter_ref[x : x + 1, side * HALF : (side + 1) * HALF] = total


vmem = pl.BlockSpec(memory_space=pltpu.VMEM)
hbm = pl.BlockSpec(memory_space=pltpu.HBM)
smem = pl.BlockSpec(memory_space=pltpu.SMEM)
params = pltpu.CompilerParams(vmem_limit_bytes=32 * 1024 * 1024)


def like(shape, dtype=f32):
    return jax.ShapeDtypeStruct(shape, dtype)


def body(inputs, short_weights, filters, skip, grad_out):
    points, strip, turn = [jnp.asarray(values) for values in tables()]
    message = pl.pallas_call(
        pack_kernel,
        out_shape=like((BLOCKS, 4, 3 * HALF), bf16),
        in_specs=[hbm] * 3,
        out_specs=vmem,
        scratch_shapes=[
            pltpu.VMEM((3, FILTERS, SPAN), bf16),
            pltpu.VMEM((FILTERS, SPAN), bf16),
            pltpu.VMEM((FILTERS, SPAN), f32),
            pltpu.VMEM((FILTERS, 4, 3 * HALF), f32),
            pltpu.VMEM((FILTERS, 4, 3 * HALF), bf16),
            pltpu.SemaphoreType.DMA((3,)),
        ],
        compiler_params=params,
    )(*[pltpu.with_memory_space_constraint(x, pltpu.HBM) for x in (inputs, grad_out, filters)])
    data = lax.all_to_all(message, "seq", split_axis=0, concat_axis=0, tiled=True)
    corr, spec = pl.pallas_call(
        corr_kernel,
        out_shape=(like((BLOCKS, HALF)), like((8 * BLOCKS, HALF))),
        in_specs=[vmem, smem, smem] + [vmem] * 3,
        out_specs=(vmem,) * 2,
        scratch_shapes=[pltpu.VMEM((BLOCKS, 4, 3 * HALF), f32)],
        compiler_params=params,
    )(data, short_weights, skip, points, strip, turn)
    corr = lax.ppermute(corr, ("seq", "chan"), owner_route())
    answer = pl.pallas_call(
        channel_kernel,
        out_shape=like((FILTERS * ROWS, HALF)),
        in_specs=[vmem, smem, smem] + [vmem] * 4,
        out_specs=vmem,
        scratch_shapes=[pltpu.VMEM((BLOCKS, 4, 3 * HALF), f32)],
        compiler_params=params,
        cost_estimate=pl.CostEstimate(flops=10**9, bytes_accessed=4 * 10**6, transcendentals=0),
    )(data, short_weights, skip, points, strip, turn, spec)
    answer = pl.pallas_call(
        merge_kernel,
        out_shape=like((FILTERS * ROWS, HALF)),
        in_specs=[vmem] * 2,
        out_specs=vmem,
        compiler_params=params,
    )(answer, corr)
    answer = lax.all_to_all(
        answer.reshape(FILTERS, 1, ROWS * HALF),
        "seq",
        split_axis=0,
        concat_axis=0,
        tiled=True,
        axis_index_groups=PARTNERS,
    ).reshape(FILTERS * ROWS, HALF)
    grads, skip_grad, short_grad, filter_grad = pl.pallas_call(
        place_kernel,
        out_shape=(
            like((3, FILTERS, SPAN)),
            like((1, FILTERS)),
            like((3, TAPS, FILTERS)),
            like((4, SPAN)),
        ),
        in_specs=[vmem],
        out_specs=(vmem,) * 4,
        scratch_shapes=[pltpu.VMEM((FILTERS, HALF), f32)],
        compiler_params=params,
    )(answer)
    return grads, filter_grad, skip_grad.reshape(FILTERS), short_grad


def solution(mesh):
    placed = (
        P(None, "chan", "seq"),
        P(None, None, "chan"),
        P(None, "seq"),
        P("chan"),
        P("chan", "seq"),
    )
    return jax.shard_map(
        body,
        mesh=mesh,
        in_specs=placed,
        out_specs=(P(None, "chan", "seq"), P("chan", "seq"), P("chan"), P(None, None, "chan")),
        check_vma=False,
    )
```

time: 63 us -> 59.5 us (0.944)
  the two profiles are of different devices: /device:TPU:1 before, /device:TPU:8 now
where the time goes in v7:
time: 59.5 us; the launch traced here: 59.3 us
  blocking collectives  52.5 us (88%)
  Pallas kernels  5.36 us (9%)
  between operations  0.73 us (1%)
  starting transfers between devices  0.66 us (1%)
    all_to_all x1, blocking collectives, body(): lax.all_to_all(message, 'seq', split_axis=0, concat_axis=0, tiled=True)  34.7 us
    all_to_all x1, blocking collectives, body(): lax.all_to_all(answer.reshape(FILTERS, 1, ROWS * HALF), 'seq', split_axis...  17.8 us
    pallas_call x1, Pallas kernels, body(): pl.pallas_call(channel_kernel, out_shape=like((FILTERS * ROWS, HALF)), in...  1.88 us
    pallas_call x1, Pallas kernels, body(): pl.pallas_call(corr_kernel, out_shape=(like((BLOCKS, HALF)), like((8 * BL...  1.76 us
  transfers between devices with their start and end apart: 1, of which 0 were waited for; matrix products, arithmetic and copies ran while one was open for 0% of the time, Pallas kernels for 3%

profile of v7, /device:TPU:8, one launch (start us, length us, event | category | flops | bytes accessed | tf_op | source)
XLA Modules:
  0.0 59.3 jit_solution(16801176754869799444)
XLA Ops:
  0.6 1.0 %shard_map.111 = bf16[64,4,384]{2,1,0:T(4,128)(2,1)S(1)} custom-call(bf16[3,32,256]{2,1,0:T(8,128)(2,1)} %inputs_hbm.1, bf16[32,256]{1,0:T(8,128)(2,1)} %grad_hbm.1, f32[32,256]{1,0:T(8,128)} %filters_hbm.1), custom_call_target="tpu_custom_call" | custom-call | tf_op jit(solution)/shard_map/pallas_call | solution.py:364
  1.6 0.0 copy-start
  1.6 0.0 copy-start.1
  1.7 0.0 copy-start.2
  1.7 0.0 copy-start.3
  1.7 0.0 copy-start.4
  1.7 34.7 %all_to_all.10.data_ref = bf16[64,4,384]{2,1,0:T(4,128)(2,1)S(1)} all-to-all(bf16[64,4,384]{2,1,0:T(4,128)(2,1)S(1)} %shard_map.111), channel_id=1, replica_groups=mesh['seq'=64,'chan'=8] {'seq'}, dimensions={0} | all-to-all | bytes 393216 | tf_op jit(solution)/shard_map/all_to_all | solution.py:379
  36.4 0.0 copy-done
  36.4 0.0 copy-done.1
  36.4 0.0 copy-done.2
  36.4 0.0 copy-done.3
  36.5 0.0 copy-done.4
  36.5 1.8 %shard_map.112 = (f32[64,128]{1,0:T(8,128)S(1)}, f32[512,128]{1,0:T(8,128)S(1)}) custom-call(bf16[64,4,384]{2,1,0:T(4,128)(2,1)S(1)} %all_to_all.10.data_ref, f32[3,3,32]{2,1,0:T(4,128)S(1)} %copy-done.3, f32[32]{0:T(128)S(1)} %copy-done.4, bf16[384,256]{1,0:T(8,128)(2,1)S(1)} %copy-done, bf16[192,256]{1,0:T(8,128)(2,1)S(1)} %copy-done.1, ...), custom_call_target="tpu_custom_call" | custom-call | tf_op jit(solution)/shard_map/pallas_call | solution.py:380
  38.2 0.7 %collective-permute-start = (f32[64,128]{1,0:T(8,128)S(1)}, f32[64,128]{1,0:T(8,128)S(1)}, u32[]{:S(2)}, u32[]{:S(2)}) collective-permute-start(f32[64,128]{1,0:T(8,128)S(1)} %get-tuple-element.11), channel_id=1, source_target_pairs={{0,0},{1,1},{2,2},{3,3},{4,4},{5,5},{6,6},{7,7},{8,9},{9,8},{10,11... | collective-permute-start | bytes 98312 | tf_op jit(solution)/shard_map/ppermute | solution.py:388
  38.9 1.9 %shard_map.113.answer_ref = f32[288,128]{1,0:T(8,128)S(1)} custom-call(bf16[64,4,384]{2,1,0:T(4,128)(2,1)S(1)} %all_to_all.10.data_ref, f32[3,3,32]{2,1,0:T(4,128)S(1)} %copy-done.3, f32[32]{0:T(128)S(1)} %copy-done.4, bf16[384,256]{1,0:T(8,128)(2,1)S(1)} %copy-done, bf16[192,256]{1,0:T(8,128)(2,1)S(1)} %copy-done.1, f32[40,256]{1,0:T(8,128)S(1)} %copy-done.2, ...), custom_call_target="tpu_custom_call" | custom-call | flops 1000000000 | bytes 4000000 | tf_op jit(solution)/shard_map/pallas_call | solution.py:389
  40.8 0.0 collective-permute-done.corr_ref
  40.8 17.8 %all_to_all.11 = f32[32,1,1152]{2,1,0:T(1,128)S(1)} all-to-all(f32[32,1,1152]{2,1,0:T(1,128)S(1)} %bitcast.4), channel_id=1, replica_groups={{0,8,16,24,32,40,48,56,128,136,144,152,160,168,176,184,256,264,272,280,..., dimensions={0} | all-to-all | bytes 294912 | tf_op jit(solution)/shard_map/all_to_all | solution.py:405
  58.6 0.7 %shard_map.115 = (f32[3,32,256]{2,1,0:T(8,128)}, f32[1,32]{1,0:T(1,128)}, f32[3,3,32]{2,1,0:T(4,128)}, f32[4,256]{1,0:T(4,128)}) custom-call(f32[288,128]{1,0:T(8,128)S(1)} %bitcast.3), custom_call_target="tpu_custom_call" | custom-call | tf_op jit(solution)/shard_map/pallas_call | solution.py:413
  (1 shorter events, 0.0 us)
Async XLA Ops:
  1.6 34.8 %copy-start = (bf16[384,256]{1,0:T(8,128)(2,1)S(1)}, bf16[384,256]{1,0:T(8,128)(2,1)}, u32[]{:S(2)}) copy-start(bf16[384,256]{1,0:T(8,128)(2,1)} %constant.6.clone.points_ref) | copy-start | bytes 589828
  1.6 34.8 %copy-start.1 = (bf16[192,256]{1,0:T(8,128)(2,1)S(1)}, bf16[192,256]{1,0:T(8,128)(2,1)}, u32[]{:S(2)}) copy-start(bf16[192,256]{1,0:T(8,128)(2,1)} %constant.7.clone.strip_ref) | copy-start | bytes 294916
  1.7 34.8 %copy-start.2 = (f32[40,256]{1,0:T(8,128)S(1)}, f32[40,256]{1,0:T(8,128)}, u32[]{:S(2)}) copy-start(f32[40,256]{1,0:T(8,128)} %constant.8.clone.turn_ref) | copy-start | bytes 122884
  1.7 34.8 %copy-start.3 = (f32[3,3,32]{2,1,0:T(4,128)S(1)}, f32[3,3,32]{2,1,0:T(4,128)}, u32[]{:S(2)}) copy-start(f32[3,3,32]{2,1,0:T(4,128)} %taps_ref.3) | copy-start | bytes 3460
  1.7 34.8 %copy-start.4 = (f32[32]{0:T(128)S(1)}, f32[32]{0:T(128)}, u32[]{:S(2)}) copy-start(f32[32]{0:T(128)} %skip_ref.3) | copy-start | bytes 388
  38.2 2.6 %collective-permute-start = (f32[64,128]{1,0:T(8,128)S(1)}, f32[64,128]{1,0:T(8,128)S(1)}, u32[]{:S(2)}, u32[]{:S(2)}) collective-permute-start(f32[64,128]{1,0:T(8,128)S(1)} %get-tuple-element.11), channel_id=1, source_target_pairs={{0,0},{1,1},{2,2},{3,3},{4,4},{5,5},{6,6},{7,7},{8,9},{9,8},{10,11... | collective-permute-start | bytes 98312 | tf_op jit(solution)/shard_map/ppermute | solution.py:388

commit v8 on v7

--- a/solution.py
+++ b/solution.py
@@ -63,13 +63,10 @@
     strip = np.zeros((3 * BLOCKS, SPAN), dtype=jnp.bfloat16)
     strip[: 2 * BLOCKS, : 3 * BLOCKS] = forward_rows
     strip[2 * BLOCKS :] = inverse_rows
-    eight = np.arange(8)
-    coarse = 2 * math.pi * (32 * eight[:, None] * cols[None, :]) / (4.0 * TOTAL)
-    fine = 2 * math.pi * ((4 * eight + 1)[:, None] * cols[None, :]) / (4.0 * TOTAL)
+    full = 2 * math.pi * (odd[:, None] * cols[None, :]) / (4.0 * TOTAL)
     step = 2 * math.pi * near / SPAN
     step = np.concatenate([np.cos(step), np.sin(step)])[None, :] * np.ones((8, 1))
-    turn = np.concatenate([np.cos(coarse), np.sin(coarse), np.cos(fine), np.sin(fine), step])
-    turn = turn.astype(np.float32)
+    turn = np.concatenate([np.cos(full), np.sin(full), step]).astype(np.float32)
     return points, strip, turn
 
 
@@ -141,26 +138,23 @@
     return jnp.sum(jnp.sum(x, axis=0, keepdims=True), axis=1, keepdims=True)
 
 
-def turns(turn_ref):
-    cosines, sines = [], []
-    fine_cos, fine_sin = turn_ref[16:24, :], turn_ref[24:32, :]
-    for a in range(8):
-        coarse_cos, coarse_sin = turn_ref[a : a + 1, :], turn_ref[8 + a : 9 + a, :]
-        cosines.append(coarse_cos * fine_cos - coarse_sin * fine_sin)
-        sines.append(coarse_sin * fine_cos + coarse_cos * fine_sin)
-    return jnp.concatenate(cosines, axis=0), jnp.concatenate(sines, axis=0)
-
-
 def seat():
     place, g = lax.axis_index("seq"), lax.axis_index("chan")
     owner = jnp.bitwise_xor(lax.rem(place, RUN), g)
     return g, owner, 4 * owner + place // (2 * RUN), lax.rem(place // RUN, 2)
 
 
-def unpack(data_ref, rows_ref):
-    rows_ref[...] = data_ref[...].astype(f32)
+def own_taps(taps_ref, channel):
+    lane = lax.broadcasted_iota(jnp.int32, taps_ref.shape, 2)
+    own = jnp.sum(jnp.where(lane == channel, taps_ref[...], 0.0), axis=2, keepdims=True)
+    return [[own[b, j : j + 1, :] for j in range(TAPS)] for b in range(3)]
+
+
+def unpack(data_ref, rows_ref, count):
+    width = count // 2 * HALF
+    rows_ref[:, :, :width] = data_ref[:, :, :width].astype(f32)
     parts = []
-    for i in range(6):
+    for i in range(count):
         pieces = []
         for side in range(2):
             row, tile = place_of(2 * i + side)
@@ -182,8 +176,9 @@
     left = strip_ref[: 2 * BLOCKS, : 3 * BLOCKS]
     right = strip_ref[2 * BLOCKS :, :]
     right = jnp.concatenate([right[:, :HALF], right], axis=1)
-    odd = turn_ref[32:33, :HALF], turn_ref[32:33, HALF:]
-    return left, right, turns(turn_ref), odd
+    last = 2 * BLOCKS
+    odd = turn_ref[last : last + 1, :HALF], turn_ref[last : last + 1, HALF:]
+    return left, right, (turn_ref[:BLOCKS, :], turn_ref[BLOCKS:last, :]), odd
 
 
 def pair(values, i):
@@ -252,8 +247,8 @@
     data_ref, taps_ref, skip_ref, points_ref, strip_ref, turn_ref, corr_ref, spec_ref, rows_ref
 ):
     g, owner, channel, b_own = seat()
-    parts = unpack(data_ref, rows_ref)
-    taps = [[taps_ref[b, j, channel] for j in range(TAPS)] for b in range(3)]
+    parts = unpack(data_ref, rows_ref, 4)
+    taps = own_taps(taps_ref, channel)
     _, (query, key, value) = mix(parts[:3], taps)
     product, dw = key * value, parts[3] * query
     left, right, turn, odd = constants(strip_ref, turn_ref)
@@ -272,10 +267,12 @@
     data_ref, taps_ref, skip_ref, points_ref, strip_ref, turn_ref, spec_ref, out_ref, rows_ref
 ):
     _, _, channel, b_own = seat()
-    parts = unpack(data_ref, rows_ref)
+    parts = unpack(data_ref, rows_ref, 6)
     grad, h = parts[3], parts[4] + parts[5]
-    taps = [[taps_ref[b, j, channel] for j in range(TAPS)] for b in range(3)]
-    direct = skip_ref[channel]
+    taps = own_taps(taps_ref, channel)
+    lane = lax.broadcasted_iota(jnp.int32, (1, FILTERS), 1)
+    line = skip_ref[...].reshape(1, FILTERS)
+    direct = jnp.sum(jnp.where(lane == channel, line, 0.0), axis=1, keepdims=True)
     moved, (query, key, value) = mix(parts[:3], taps)
     product, dw = key * value, grad * query
     left, right, turn, odd = constants(strip_ref, turn_ref)
@@ -351,7 +348,6 @@
 
 vmem = pl.BlockSpec(memory_space=pltpu.VMEM)
 hbm = pl.BlockSpec(memory_space=pltpu.HBM)
-smem = pl.BlockSpec(memory_space=pltpu.SMEM)
 params = pltpu.CompilerParams(vmem_limit_bytes=32 * 1024 * 1024)
 
 
@@ -380,7 +376,7 @@
     corr, spec = pl.pallas_call(
         corr_kernel,
         out_shape=(like((BLOCKS, HALF)), like((8 * BLOCKS, HALF))),
-        in_specs=[vmem, smem, smem] + [vmem] * 3,
+        in_specs=[vmem] * 6,
         out_specs=(vmem,) * 2,
         scratch_shapes=[pltpu.VMEM((BLOCKS, 4, 3 * HALF), f32)],
         compiler_params=params,
@@ -389,7 +385,7 @@
     answer = pl.pallas_call(
         channel_kernel,
         out_shape=like((FILTERS * ROWS, HALF)),
-        in_specs=[vmem, smem, smem] + [vmem] * 4,
+        in_specs=[vmem] * 7,
         out_specs=vmem,
         scratch_shapes=[pltpu.VMEM((BLOCKS, 4, 3 * HALF), f32)],
         compiler_params=params,

time: 59.5 us -> 58.9 us (0.990)
  Pallas kernels: 5.36 us -> 4.11 us
  blocking collectives: 52.5 us -> 53.1 us
    pallas_call x1, Pallas kernels: 1.76 us -> 1.11 us  [body(): pl.pallas_call(corr_kernel, out_shape=(like((BLOCKS, HALF)), like((8 * BL...]
    pallas_call x1, Pallas kernels: 1.88 us -> 1.25 us  [body(): pl.pallas_call(channel_kernel, out_shape=like((FILTERS * ROWS, HALF)), in...]
    all_to_all x1, blocking collectives: 17.8 us -> 18.4 us  [body(): lax.all_to_all(answer.reshape(FILTERS, 1, ROWS * HALF), 'seq', split_axis...]
  transfers between devices with their start and end apart: 1 -> 1, of which waited for: 0 -> 0; matrix products, arithmetic and copies ran while one was open for 0% -> 0% of each run, Pallas kernels for 3% -> 2%
where the time goes in v8:
time: 58.9 us; the launch traced here: 58.7 us
  blocking collectives  53.1 us (90%)
  Pallas kernels  4.11 us (7%)
  between operations  0.74 us (1%)
  starting transfers between devices  0.66 us (1%)
    all_to_all x1, blocking collectives, body(): lax.all_to_all(message, 'seq', split_axis=0, concat_axis=0, tiled=True)  34.7 us
    all_to_all x1, blocking collectives, body(): lax.all_to_all(answer.reshape(FILTERS, 1, ROWS * HALF), 'seq', split_axis...  18.4 us
    pallas_call x1, Pallas kernels, body(): pl.pallas_call(channel_kernel, out_shape=like((FILTERS * ROWS, HALF)), in...  1.25 us
  transfers between devices with their start and end apart: 1, of which 0 were waited for; matrix products, arithmetic and copies ran while one was open for 0% of the time, Pallas kernels for 2%

profile of v8, /device:TPU:8, one launch (start us, length us, event | category | flops | bytes accessed | tf_op | source)
XLA Modules:
  0.0 58.7 jit_solution(3173158124587901831)
XLA Ops:
  0.6 0.0 copy-start.2
  0.6 1.0 %shard_map.111 = bf16[64,4,384]{2,1,0:T(4,128)(2,1)S(1)} custom-call(bf16[3,32,256]{2,1,0:T(8,128)(2,1)} %inputs_hbm.1, bf16[32,256]{1,0:T(8,128)(2,1)} %grad_hbm.1, f32[32,256]{1,0:T(8,128)} %filters_hbm.1), custom_call_target="tpu_custom_call" | custom-call | tf_op jit(solution)/shard_map/pallas_call | solution.py:360
  1.7 0.0 copy-start
  1.7 0.0 copy-start.1
  1.7 0.0 copy-start.3
  1.7 0.0 copy-start.4
  1.7 34.7 %all_to_all.10.data_ref = bf16[64,4,384]{2,1,0:T(4,128)(2,1)S(1)} all-to-all(bf16[64,4,384]{2,1,0:T(4,128)(2,1)S(1)} %shard_map.111), channel_id=1, replica_groups=mesh['seq'=64,'chan'=8] {'seq'}, dimensions={0} | all-to-all | bytes 393216 | tf_op jit(solution)/shard_map/all_to_all | solution.py:375
  36.5 0.0 copy-done.2
  36.5 0.0 copy-done
  36.5 0.0 copy-done.1
  36.5 0.0 copy-done.3
  36.5 0.0 copy-done.4
  36.5 1.1 %shard_map.112 = (f32[64,128]{1,0:T(8,128)S(1)}, f32[512,128]{1,0:T(8,128)S(1)}) custom-call(bf16[64,4,384]{2,1,0:T(4,128)(2,1)S(1)} %all_to_all.10.data_ref, f32[3,3,32]{2,1,0:T(4,128)S(1)} %copy-done.3, f32[32]{0:T(128)S(1)} %copy-done.4, bf16[384,256]{1,0:T(8,128)(2,1)S(1)} %copy-done, bf16[192,256]{1,0:T(8,128)(2,1)S(1)} %copy-done.2, ...), custom_call_target="tpu_custom_call" | custom-call | tf_op jit(solution)/shard_map/pallas_call | solution.py:376
  37.6 0.7 %collective-permute-start = (f32[64,128]{1,0:T(8,128)S(1)}, f32[64,128]{1,0:T(8,128)S(1)}, u32[]{:S(2)}, u32[]{:S(2)}) collective-permute-start(f32[64,128]{1,0:T(8,128)S(1)} %get-tuple-element.11), channel_id=1, source_target_pairs={{0,0},{1,1},{2,2},{3,3},{4,4},{5,5},{6,6},{7,7},{8,9},{9,8},{10,11... | collective-permute-start | bytes 98312 | tf_op jit(solution)/shard_map/ppermute | solution.py:384
  38.3 1.2 %shard_map.113.answer_ref = f32[288,128]{1,0:T(8,128)S(1)} custom-call(bf16[64,4,384]{2,1,0:T(4,128)(2,1)S(1)} %all_to_all.10.data_ref, f32[3,3,32]{2,1,0:T(4,128)S(1)} %copy-done.3, f32[32]{0:T(128)S(1)} %copy-done.4, bf16[384,256]{1,0:T(8,128)(2,1)S(1)} %copy-done, bf16[192,256]{1,0:T(8,128)(2,1)S(1)} %copy-done.2, f32[136,256]{1,0:T(8,128)S(1)} %copy-done.1, ...), custom_call_target="tpu_custom_call" | custom-call | flops 1000000000 | bytes 4000000 | tf_op jit(solution)/shard_map/pallas_call | solution.py:385
  39.5 0.0 collective-permute-done.corr_ref
  39.6 18.4 %all_to_all.11 = f32[32,1,1152]{2,1,0:T(1,128)S(1)} all-to-all(f32[32,1,1152]{2,1,0:T(1,128)S(1)} %bitcast.4), channel_id=1, replica_groups={{0,8,16,24,32,40,48,56,128,136,144,152,160,168,176,184,256,264,272,280,..., dimensions={0} | all-to-all | bytes 294912 | tf_op jit(solution)/shard_map/all_to_all | solution.py:401
  58.0 0.7 %shard_map.115 = (f32[3,32,256]{2,1,0:T(8,128)}, f32[1,32]{1,0:T(1,128)}, f32[3,3,32]{2,1,0:T(4,128)}, f32[4,256]{1,0:T(4,128)}) custom-call(f32[288,128]{1,0:T(8,128)S(1)} %bitcast.3), custom_call_target="tpu_custom_call" | custom-call | tf_op jit(solution)/shard_map/pallas_call | solution.py:409
  (1 shorter events, 0.0 us)
Async XLA Ops:
  0.6 35.8 %copy-start.2 = (bf16[192,256]{1,0:T(8,128)(2,1)S(1)}, bf16[192,256]{1,0:T(8,128)(2,1)}, u32[]{:S(2)}) copy-start(bf16[192,256]{1,0:T(8,128)(2,1)} %constant.7.clone.strip_ref) | copy-start | bytes 294916
  1.7 34.8 %copy-start = (bf16[384,256]{1,0:T(8,128)(2,1)S(1)}, bf16[384,256]{1,0:T(8,128)(2,1)}, u32[]{:S(2)}) copy-start(bf16[384,256]{1,0:T(8,128)(2,1)} %constant.6.clone.points_ref) | copy-start | bytes 589828
  1.7 34.8 %copy-start.1 = (f32[136,256]{1,0:T(8,128)S(1)}, f32[136,256]{1,0:T(8,128)}, u32[]{:S(2)}) copy-start(f32[136,256]{1,0:T(8,128)} %constant.8.clone.turn_ref) | copy-start | bytes 417796
  1.7 34.8 %copy-start.3 = (f32[3,3,32]{2,1,0:T(4,128)S(1)}, f32[3,3,32]{2,1,0:T(4,128)}, u32[]{:S(2)}) copy-start(f32[3,3,32]{2,1,0:T(4,128)} %taps_ref.3) | copy-start | bytes 3460
  1.7 34.8 %copy-start.4 = (f32[32]{0:T(128)S(1)}, f32[32]{0:T(128)}, u32[]{:S(2)}) copy-start(f32[32]{0:T(128)} %skip_ref.3) | copy-start | bytes 388
  37.6 1.9 %collective-permute-start = (f32[64,128]{1,0:T(8,128)S(1)}, f32[64,128]{1,0:T(8,128)S(1)}, u32[]{:S(2)}, u32[]{:S(2)}) collective-permute-start(f32[64,128]{1,0:T(8,128)S(1)} %get-tuple-element.11), channel_id=1, source_target_pairs={{0,0},{1,1},{2,2},{3,3},{4,4},{5,5},{6,6},{7,7},{8,9},{9,8},{10,11... | collective-permute-start | bytes 98312 | tf_op jit(solution)/shard_map/ppermute | solution.py:384

commit v9 on v8

--- a/solution.py
+++ b/solution.py
@@ -25,7 +25,9 @@
 
 
 def is_far(g, owner):
-    return abs(g // 2 - owner // 2) == 3
+    here, there = g // 2, owner // 2
+    apart = abs(here - there)
+    return (apart == 3) | ((apart == 2) & ((here == 1) | (here == 2)))
 
 
 def owner_route():

time: 58.9 us -> 58.9 us (level)
  no operation moved by 1% of the time
where the time goes in v9:
time: 58.9 us; the launch traced here: 58.7 us
  blocking collectives  53.1 us (90%)
  Pallas kernels  4.11 us (7%)
  between operations  0.74 us (1%)
  starting transfers between devices  0.66 us (1%)
    all_to_all x1, blocking collectives, body(): lax.all_to_all(message, 'seq', split_axis=0, concat_axis=0, tiled=True)  34.7 us
    all_to_all x1, blocking collectives, body(): lax.all_to_all(answer.reshape(FILTERS, 1, ROWS * HALF), 'seq', split_axis...  18.4 us
    pallas_call x1, Pallas kernels, body(): pl.pallas_call(channel_kernel, out_shape=like((FILTERS * ROWS, HALF)), in...  1.25 us
  transfers between devices with their start and end apart: 1, of which 0 were waited for; matrix products, arithmetic and copies ran while one was open for 0% of the time, Pallas kernels for 2%

profile of v9, /device:TPU:8, one launch (start us, length us, event | category | flops | bytes accessed | tf_op | source)
XLA Modules:
  0.0 58.7 jit_solution(5928626862622286809)
XLA Ops:
  0.6 0.0 copy-start.2
  0.6 1.0 %shard_map.111 = bf16[64,4,384]{2,1,0:T(4,128)(2,1)S(1)} custom-call(bf16[3,32,256]{2,1,0:T(8,128)(2,1)} %inputs_hbm.1, bf16[32,256]{1,0:T(8,128)(2,1)} %grad_hbm.1, f32[32,256]{1,0:T(8,128)} %filters_hbm.1), custom_call_target="tpu_custom_call" | custom-call | tf_op jit(solution)/shard_map/pallas_call | solution.py:362
  1.7 0.0 copy-start
  1.7 0.0 copy-start.1
  1.7 0.0 copy-start.3
  1.7 0.0 copy-start.4
  1.7 34.7 %all_to_all.10.data_ref = bf16[64,4,384]{2,1,0:T(4,128)(2,1)S(1)} all-to-all(bf16[64,4,384]{2,1,0:T(4,128)(2,1)S(1)} %shard_map.111), channel_id=1, replica_groups=mesh['seq'=64,'chan'=8] {'seq'}, dimensions={0} | all-to-all | bytes 393216 | tf_op jit(solution)/shard_map/all_to_all | solution.py:377
  36.5 0.0 copy-done.2
  36.5 0.0 copy-done
  36.5 0.0 copy-done.1
  36.5 0.0 copy-done.3
  36.5 0.0 copy-done.4
  36.5 1.1 %shard_map.112 = (f32[64,128]{1,0:T(8,128)S(1)}, f32[512,128]{1,0:T(8,128)S(1)}) custom-call(bf16[64,4,384]{2,1,0:T(4,128)(2,1)S(1)} %all_to_all.10.data_ref, f32[3,3,32]{2,1,0:T(4,128)S(1)} %copy-done.3, f32[32]{0:T(128)S(1)} %copy-done.4, bf16[384,256]{1,0:T(8,128)(2,1)S(1)} %copy-done, bf16[192,256]{1,0:T(8,128)(2,1)S(1)} %copy-done.2, ...), custom_call_target="tpu_custom_call" | custom-call | tf_op jit(solution)/shard_map/pallas_call | solution.py:378
  37.6 0.7 %collective-permute-start = (f32[64,128]{1,0:T(8,128)S(1)}, f32[64,128]{1,0:T(8,128)S(1)}, u32[]{:S(2)}, u32[]{:S(2)}) collective-permute-start(f32[64,128]{1,0:T(8,128)S(1)} %get-tuple-element.11), channel_id=1, source_target_pairs={{0,0},{1,1},{2,2},{3,3},{4,4},{5,5},{6,6},{7,7},{8,9},{9,8},{10,11... | collective-permute-start | bytes 98312 | tf_op jit(solution)/shard_map/ppermute | solution.py:386
  38.3 1.2 %shard_map.113.answer_ref = f32[288,128]{1,0:T(8,128)S(1)} custom-call(bf16[64,4,384]{2,1,0:T(4,128)(2,1)S(1)} %all_to_all.10.data_ref, f32[3,3,32]{2,1,0:T(4,128)S(1)} %copy-done.3, f32[32]{0:T(128)S(1)} %copy-done.4, bf16[384,256]{1,0:T(8,128)(2,1)S(1)} %copy-done, bf16[192,256]{1,0:T(8,128)(2,1)S(1)} %copy-done.2, f32[136,256]{1,0:T(8,128)S(1)} %copy-done.1, ...), custom_call_target="tpu_custom_call" | custom-call | flops 1000000000 | bytes 4000000 | tf_op jit(solution)/shard_map/pallas_call | solution.py:387
  39.5 0.0 collective-permute-done.corr_ref
  39.6 18.4 %all_to_all.11 = f32[32,1,1152]{2,1,0:T(1,128)S(1)} all-to-all(f32[32,1,1152]{2,1,0:T(1,128)S(1)} %bitcast.4), channel_id=1, replica_groups={{0,8,16,24,32,40,48,56,128,136,144,152,160,168,176,184,256,264,272,280,..., dimensions={0} | all-to-all | bytes 294912 | tf_op jit(solution)/shard_map/all_to_all | solution.py:403
  58.0 0.7 %shard_map.115 = (f32[3,32,256]{2,1,0:T(8,128)}, f32[1,32]{1,0:T(1,128)}, f32[3,3,32]{2,1,0:T(4,128)}, f32[4,256]{1,0:T(4,128)}) custom-call(f32[288,128]{1,0:T(8,128)S(1)} %bitcast.3), custom_call_target="tpu_custom_call" | custom-call | tf_op jit(solution)/shard_map/pallas_call | solution.py:411
  (1 shorter events, 0.0 us)
Async XLA Ops:
  0.6 35.8 %copy-start.2 = (bf16[192,256]{1,0:T(8,128)(2,1)S(1)}, bf16[192,256]{1,0:T(8,128)(2,1)}, u32[]{:S(2)}) copy-start(bf16[192,256]{1,0:T(8,128)(2,1)} %constant.7.clone.strip_ref) | copy-start | bytes 294916
  1.7 34.8 %copy-start = (bf16[384,256]{1,0:T(8,128)(2,1)S(1)}, bf16[384,256]{1,0:T(8,128)(2,1)}, u32[]{:S(2)}) copy-start(bf16[384,256]{1,0:T(8,128)(2,1)} %constant.6.clone.points_ref) | copy-start | bytes 589828
  1.7 34.8 %copy-start.1 = (f32[136,256]{1,0:T(8,128)S(1)}, f32[136,256]{1,0:T(8,128)}, u32[]{:S(2)}) copy-start(f32[136,256]{1,0:T(8,128)} %constant.8.clone.turn_ref) | copy-start | bytes 417796
  1.7 34.8 %copy-start.3 = (f32[3,3,32]{2,1,0:T(4,128)S(1)}, f32[3,3,32]{2,1,0:T(4,128)}, u32[]{:S(2)}) copy-start(f32[3,3,32]{2,1,0:T(4,128)} %taps_ref.3) | copy-start | bytes 3460
  1.7 34.8 %copy-start.4 = (f32[32]{0:T(128)S(1)}, f32[32]{0:T(128)}, u32[]{:S(2)}) copy-start(f32[32]{0:T(128)} %skip_ref.3) | copy-start | bytes 388
  37.6 1.9 %collective-permute-start = (f32[64,128]{1,0:T(8,128)S(1)}, f32[64,128]{1,0:T(8,128)S(1)}, u32[]{:S(2)}, u32[]{:S(2)}) collective-permute-start(f32[64,128]{1,0:T(8,128)S(1)} %get-tuple-element.11), channel_id=1, source_target_pairs={{0,0},{1,1},{2,2},{3,3},{4,4},{5,5},{6,6},{7,7},{8,9},{9,8},{10,11... | collective-permute-start | bytes 98312 | tf_op jit(solution)/shard_map/ppermute | solution.py:386

commit v10 on v8

--- a/solution.py
+++ b/solution.py
@@ -90,7 +90,8 @@
 
 def dot_right(x, table):
     high, low = halves(x)
-    return dot(jnp.concatenate([high, low, high], axis=1), table)
+    wide = jnp.concatenate([high, low], axis=1)
+    return dot(wide, table[: 2 * HALF]) + dot(high, table[2 * HALF :])
 
 
 def later(x, n):
@@ -118,17 +119,24 @@
     ]
     for copy in copies:
         copy.start()
-    for copy in copies:
-        copy.wait()
-    h = filters_ref[...]
-    h_high = h.astype(bf16).astype(f32)
-    parts = [inputs_ref[b].astype(f32) for b in range(3)]
-    parts += [grad_ref[...].astype(f32), h_high, h - h_high]
-    for i, part in enumerate(parts):
+
+    def put(i, part):
         for side in range(2):
             row, tile = place_of(2 * i + side)
             rows_ref[:, row, tile] = part[:, side * HALF : (side + 1) * HALF]
-    short_ref[...] = rows_ref[...].astype(bf16)
+
+    copies[2].wait()
+    h = filters_ref[...]
+    h_high = h.astype(bf16).astype(f32)
+    put(4, h_high)
+    put(5, h - h_high)
+    copies[1].wait()
+    put(3, grad_ref[...].astype(f32))
+    short_ref[:, :, 2 * HALF :] = rows_ref[:, :, 2 * HALF :].astype(bf16)
+    copies[0].wait()
+    for b in range(3):
+        put(b, inputs_ref[b].astype(f32))
+    short_ref[:, :, : 2 * HALF] = rows_ref[:, :, : 2 * HALF].astype(bf16)
     g = lax.axis_index("chan")
     for place in range(BLOCKS):
         out_ref[place] = short_ref[4 * jnp.bitwise_xor(g, place % RUN) + place // (2 * RUN)]

time: 58.9 us -> 58.9 us (level)
  no operation moved by 1% of the time
where the time goes in v10:
time: 58.9 us; the launch traced here: 58.6 us
  blocking collectives  53.1 us (90%)
  Pallas kernels  4.08 us (7%)
  between operations  0.74 us (1%)
  starting transfers between devices  0.66 us (1%)
    all_to_all x1, blocking collectives, body(): lax.all_to_all(message, 'seq', split_axis=0, concat_axis=0, tiled=True)  34.7 us
    all_to_all x1, blocking collectives, body(): lax.all_to_all(answer.reshape(FILTERS, 1, ROWS * HALF), 'seq', split_axis...  18.4 us
    pallas_call x1, Pallas kernels, body(): pl.pallas_call(channel_kernel, out_shape=like((FILTERS * ROWS, HALF)), in...  1.23 us
  transfers between devices with their start and end apart: 1, of which 0 were waited for; matrix products, arithmetic and copies ran while one was open for 0% of the time, Pallas kernels for 2%

profile of v10, /device:TPU:8, one launch (start us, length us, event | category | flops | bytes accessed | tf_op | source)
XLA Modules:
  0.0 58.6 jit_solution(17089851798715401435)
XLA Ops:
  0.6 0.0 copy-start.2
  0.6 1.0 %shard_map.111 = bf16[64,4,384]{2,1,0:T(4,128)(2,1)S(1)} custom-call(bf16[3,32,256]{2,1,0:T(8,128)(2,1)} %inputs_hbm.1, bf16[32,256]{1,0:T(8,128)(2,1)} %grad_hbm.1, f32[32,256]{1,0:T(8,128)} %filters_hbm.1), custom_call_target="tpu_custom_call" | custom-call | tf_op jit(solution)/shard_map/pallas_call | solution.py:368
  1.7 0.0 copy-start
  1.7 0.0 copy-start.1
  1.7 0.0 copy-start.3
  1.7 0.0 copy-start.4
  1.7 34.7 %all_to_all.10.data_ref = bf16[64,4,384]{2,1,0:T(4,128)(2,1)S(1)} all-to-all(bf16[64,4,384]{2,1,0:T(4,128)(2,1)S(1)} %shard_map.111), channel_id=1, replica_groups=mesh['seq'=64,'chan'=8] {'seq'}, dimensions={0} | all-to-all | bytes 393216 | tf_op jit(solution)/shard_map/all_to_all | solution.py:383
  36.5 0.0 copy-done.2
  36.5 0.0 copy-done
  36.5 0.0 copy-done.1
  36.5 0.0 copy-done.3
  36.5 0.0 copy-done.4
  36.5 1.1 %shard_map.112 = (f32[64,128]{1,0:T(8,128)S(1)}, f32[512,128]{1,0:T(8,128)S(1)}) custom-call(bf16[64,4,384]{2,1,0:T(4,128)(2,1)S(1)} %all_to_all.10.data_ref, f32[3,3,32]{2,1,0:T(4,128)S(1)} %copy-done.3, f32[32]{0:T(128)S(1)} %copy-done.4, bf16[384,256]{1,0:T(8,128)(2,1)S(1)} %copy-done, bf16[192,256]{1,0:T(8,128)(2,1)S(1)} %copy-done.2, ...), custom_call_target="tpu_custom_call" | custom-call | tf_op jit(solution)/shard_map/pallas_call | solution.py:384
  37.6 0.7 %collective-permute-start = (f32[64,128]{1,0:T(8,128)S(1)}, f32[64,128]{1,0:T(8,128)S(1)}, u32[]{:S(2)}, u32[]{:S(2)}) collective-permute-start(f32[64,128]{1,0:T(8,128)S(1)} %get-tuple-element.11), channel_id=1, source_target_pairs={{0,0},{1,1},{2,2},{3,3},{4,4},{5,5},{6,6},{7,7},{8,9},{9,8},{10,11... | collective-permute-start | bytes 98312 | tf_op jit(solution)/shard_map/ppermute | solution.py:392
  38.3 1.2 %shard_map.113.answer_ref = f32[288,128]{1,0:T(8,128)S(1)} custom-call(bf16[64,4,384]{2,1,0:T(4,128)(2,1)S(1)} %all_to_all.10.data_ref, f32[3,3,32]{2,1,0:T(4,128)S(1)} %copy-done.3, f32[32]{0:T(128)S(1)} %copy-done.4, bf16[384,256]{1,0:T(8,128)(2,1)S(1)} %copy-done, bf16[192,256]{1,0:T(8,128)(2,1)S(1)} %copy-done.2, f32[136,256]{1,0:T(8,128)S(1)} %copy-done.1, ...), custom_call_target="tpu_custom_call" | custom-call | flops 1000000000 | bytes 4000000 | tf_op jit(solution)/shard_map/pallas_call | solution.py:393
  39.5 0.0 collective-permute-done.corr_ref
  39.5 18.4 %all_to_all.11 = f32[32,1,1152]{2,1,0:T(1,128)S(1)} all-to-all(f32[32,1,1152]{2,1,0:T(1,128)S(1)} %bitcast.4), channel_id=1, replica_groups={{0,8,16,24,32,40,48,56,128,136,144,152,160,168,176,184,256,264,272,280,..., dimensions={0} | all-to-all | bytes 294912 | tf_op jit(solution)/shard_map/all_to_all | solution.py:409
  57.9 0.7 %shard_map.115 = (f32[3,32,256]{2,1,0:T(8,128)}, f32[1,32]{1,0:T(1,128)}, f32[3,3,32]{2,1,0:T(4,128)}, f32[4,256]{1,0:T(4,128)}) custom-call(f32[288,128]{1,0:T(8,128)S(1)} %bitcast.3), custom_call_target="tpu_custom_call" | custom-call | tf_op jit(solution)/shard_map/pallas_call | solution.py:417
  (1 shorter events, 0.0 us)
Async XLA Ops:
  0.6 35.8 %copy-start.2 = (bf16[192,256]{1,0:T(8,128)(2,1)S(1)}, bf16[192,256]{1,0:T(8,128)(2,1)}, u32[]{:S(2)}) copy-start(bf16[192,256]{1,0:T(8,128)(2,1)} %constant.7.clone.strip_ref) | copy-start | bytes 294916
  1.7 34.8 %copy-start = (bf16[384,256]{1,0:T(8,128)(2,1)S(1)}, bf16[384,256]{1,0:T(8,128)(2,1)}, u32[]{:S(2)}) copy-start(bf16[384,256]{1,0:T(8,128)(2,1)} %constant.6.clone.points_ref) | copy-start | bytes 589828
  1.7 34.8 %copy-start.1 = (f32[136,256]{1,0:T(8,128)S(1)}, f32[136,256]{1,0:T(8,128)}, u32[]{:S(2)}) copy-start(f32[136,256]{1,0:T(8,128)} %constant.8.clone.turn_ref) | copy-start | bytes 417796
  1.7 34.8 %copy-start.3 = (f32[3,3,32]{2,1,0:T(4,128)S(1)}, f32[3,3,32]{2,1,0:T(4,128)}, u32[]{:S(2)}) copy-start(f32[3,3,32]{2,1,0:T(4,128)} %taps_ref.3) | copy-start | bytes 3460
  1.7 34.8 %copy-start.4 = (f32[32]{0:T(128)S(1)}, f32[32]{0:T(128)}, u32[]{:S(2)}) copy-start(f32[32]{0:T(128)} %skip_ref.3) | copy-start | bytes 388
  37.6 1.9 %collective-permute-start = (f32[64,128]{1,0:T(8,128)S(1)}, f32[64,128]{1,0:T(8,128)S(1)}, u32[]{:S(2)}, u32[]{:S(2)}) collective-permute-start(f32[64,128]{1,0:T(8,128)S(1)} %get-tuple-element.11), channel_id=1, source_target_pairs={{0,0},{1,1},{2,2},{3,3},{4,4},{5,5},{6,6},{7,7},{8,9},{9,8},{10,11... | collective-permute-start | bytes 98312 | tf_op jit(solution)/shard_map/ppermute | solution.py:392

commit v11 on v8

--- a/solution.py
+++ b/solution.py
@@ -215,7 +215,7 @@
     return a[0] * b[0] + a[1] * b[1], a[1] * b[0] - a[0] * b[1]
 
 
-def inverse(spectrums, points, right, turn, odd):
+def inverse(spectrums, points, right, turn, odd, b=None):
     cosine, sine = turn
     odd_cos, odd_sin = odd
     joined = [x for spectrum in spectrums for part in spectrum for x in part]
@@ -232,6 +232,8 @@
         turned.append(
             jnp.concatenate([b_re * cosine - b_im * sine, b_im * cosine + b_re * sine], axis=0)
         )
+    if b is not None:
+        right = every_second_run(right.astype(f32), b).astype(bf16)
     return dot_left(right, jnp.concatenate(turned, axis=1))
 
 
@@ -256,9 +258,9 @@
     p, d = spectra([product, dw], points, left, turn, odd)
     for i, x in enumerate([x for spectrum in (p, d) for part in spectrum for x in part]):
         spec_ref[i * BLOCKS : (i + 1) * BLOCKS, :] = x
-    corr = inverse([[times_conj(d[e], p[e]) for e in range(2)]], points, right, turn, odd)
     b_there = jnp.where(is_far(g, owner), 1 - b_own, b_own)
-    corr = every_second_run(corr, b_there)
+    product_spec = [times_conj(d[e], p[e]) for e in range(2)]
+    corr = inverse([product_spec], points, right, turn, odd, b_there)
     for side in range(2):
         corr_ref[side * FILTERS : (side + 1) * FILTERS, :] = corr[:, side * HALF : (side + 1) * HALF]
 

time: 58.9 us -> 58.9 us (level)
  no operation moved by 1% of the time
where the time goes in v11:
time: 58.9 us; the launch traced here: 58.6 us
  blocking collectives  53.1 us (90%)
  Pallas kernels  4.1 us (7%)
  between operations  0.73 us (1%)
  starting transfers between devices  0.66 us (1%)
    all_to_all x1, blocking collectives, body(): lax.all_to_all(message, 'seq', split_axis=0, concat_axis=0, tiled=True)  34.7 us
    all_to_all x1, blocking collectives, body(): lax.all_to_all(answer.reshape(FILTERS, 1, ROWS * HALF), 'seq', split_axis...  18.4 us
    pallas_call x1, Pallas kernels, body(): pl.pallas_call(channel_kernel, out_shape=like((FILTERS * ROWS, HALF)), in...  1.25 us
  transfers between devices with their start and end apart: 1, of which 0 were waited for; matrix products, arithmetic and copies ran while one was open for 0% of the time, Pallas kernels for 2%

profile of v11, /device:TPU:8, one launch (start us, length us, event | category | flops | bytes accessed | tf_op | source)
XLA Modules:
  0.0 58.6 jit_solution(17191422820130366923)
XLA Ops:
  0.6 0.0 copy-start.2
  0.6 1.0 %shard_map.111 = bf16[64,4,384]{2,1,0:T(4,128)(2,1)S(1)} custom-call(bf16[3,32,256]{2,1,0:T(8,128)(2,1)} %inputs_hbm.1, bf16[32,256]{1,0:T(8,128)(2,1)} %grad_hbm.1, f32[32,256]{1,0:T(8,128)} %filters_hbm.1), custom_call_target="tpu_custom_call" | custom-call | tf_op jit(solution)/shard_map/pallas_call | solution.py:362
  1.7 0.0 copy-start
  1.7 0.0 copy-start.1
  1.7 0.0 copy-start.3
  1.7 0.0 copy-start.4
  1.7 34.7 %all_to_all.10.data_ref = bf16[64,4,384]{2,1,0:T(4,128)(2,1)S(1)} all-to-all(bf16[64,4,384]{2,1,0:T(4,128)(2,1)S(1)} %shard_map.111), channel_id=1, replica_groups=mesh['seq'=64,'chan'=8] {'seq'}, dimensions={0} | all-to-all | bytes 393216 | tf_op jit(solution)/shard_map/all_to_all | solution.py:377
  36.5 0.0 copy-done.2
  36.5 0.0 copy-done
  36.5 0.0 copy-done.1
  36.5 0.0 copy-done.3
  36.5 0.0 copy-done.4
  36.5 1.1 %shard_map.112 = (f32[64,128]{1,0:T(8,128)S(1)}, f32[512,128]{1,0:T(8,128)S(1)}) custom-call(bf16[64,4,384]{2,1,0:T(4,128)(2,1)S(1)} %all_to_all.10.data_ref, f32[3,3,32]{2,1,0:T(4,128)S(1)} %copy-done.3, f32[32]{0:T(128)S(1)} %copy-done.4, bf16[384,256]{1,0:T(8,128)(2,1)S(1)} %copy-done, bf16[192,256]{1,0:T(8,128)(2,1)S(1)} %copy-done.2, ...), custom_call_target="tpu_custom_call" | custom-call | tf_op jit(solution)/shard_map/pallas_call | solution.py:378
  37.6 0.7 %collective-permute-start = (f32[64,128]{1,0:T(8,128)S(1)}, f32[64,128]{1,0:T(8,128)S(1)}, u32[]{:S(2)}, u32[]{:S(2)}) collective-permute-start(f32[64,128]{1,0:T(8,128)S(1)} %get-tuple-element.11), channel_id=1, source_target_pairs={{0,0},{1,1},{2,2},{3,3},{4,4},{5,5},{6,6},{7,7},{8,9},{9,8},{10,11... | collective-permute-start | bytes 98312 | tf_op jit(solution)/shard_map/ppermute | solution.py:386
  38.3 1.2 %shard_map.113.answer_ref = f32[288,128]{1,0:T(8,128)S(1)} custom-call(bf16[64,4,384]{2,1,0:T(4,128)(2,1)S(1)} %all_to_all.10.data_ref, f32[3,3,32]{2,1,0:T(4,128)S(1)} %copy-done.3, f32[32]{0:T(128)S(1)} %copy-done.4, bf16[384,256]{1,0:T(8,128)(2,1)S(1)} %copy-done, bf16[192,256]{1,0:T(8,128)(2,1)S(1)} %copy-done.2, f32[136,256]{1,0:T(8,128)S(1)} %copy-done.1, ...), custom_call_target="tpu_custom_call" | custom-call | flops 1000000000 | bytes 4000000 | tf_op jit(solution)/shard_map/pallas_call | solution.py:387
  39.5 0.0 collective-permute-done.corr_ref
  39.6 18.4 %all_to_all.11 = f32[32,1,1152]{2,1,0:T(1,128)S(1)} all-to-all(f32[32,1,1152]{2,1,0:T(1,128)S(1)} %bitcast.4), channel_id=1, replica_groups={{0,8,16,24,32,40,48,56,128,136,144,152,160,168,176,184,256,264,272,280,..., dimensions={0} | all-to-all | bytes 294912 | tf_op jit(solution)/shard_map/all_to_all | solution.py:403
  57.9 0.7 %shard_map.115 = (f32[3,32,256]{2,1,0:T(8,128)}, f32[1,32]{1,0:T(1,128)}, f32[3,3,32]{2,1,0:T(4,128)}, f32[4,256]{1,0:T(4,128)}) custom-call(f32[288,128]{1,0:T(8,128)S(1)} %bitcast.3), custom_call_target="tpu_custom_call" | custom-call | tf_op jit(solution)/shard_map/pallas_call | solution.py:411
  (1 shorter events, 0.0 us)
Async XLA Ops:
  0.6 35.8 %copy-start.2 = (bf16[192,256]{1,0:T(8,128)(2,1)S(1)}, bf16[192,256]{1,0:T(8,128)(2,1)}, u32[]{:S(2)}) copy-start(bf16[192,256]{1,0:T(8,128)(2,1)} %constant.7.clone.strip_ref) | copy-start | bytes 294916
  1.7 34.8 %copy-start = (bf16[384,256]{1,0:T(8,128)(2,1)S(1)}, bf16[384,256]{1,0:T(8,128)(2,1)}, u32[]{:S(2)}) copy-start(bf16[384,256]{1,0:T(8,128)(2,1)} %constant.6.clone.points_ref) | copy-start | bytes 589828
  1.7 34.8 %copy-start.1 = (f32[136,256]{1,0:T(8,128)S(1)}, f32[136,256]{1,0:T(8,128)}, u32[]{:S(2)}) copy-start(f32[136,256]{1,0:T(8,128)} %constant.8.clone.turn_ref) | copy-start | bytes 417796
  1.7 34.8 %copy-start.3 = (f32[3,3,32]{2,1,0:T(4,128)S(1)}, f32[3,3,32]{2,1,0:T(4,128)}, u32[]{:S(2)}) copy-start(f32[3,3,32]{2,1,0:T(4,128)} %taps_ref.3) | copy-start | bytes 3460
  1.7 34.8 %copy-start.4 = (f32[32]{0:T(128)S(1)}, f32[32]{0:T(128)}, u32[]{:S(2)}) copy-start(f32[32]{0:T(128)} %skip_ref.3) | copy-start | bytes 388
  37.6 1.9 %collective-permute-start = (f32[64,128]{1,0:T(8,128)S(1)}, f32[64,128]{1,0:T(8,128)S(1)}, u32[]{:S(2)}, u32[]{:S(2)}) collective-permute-start(f32[64,128]{1,0:T(8,128)S(1)} %get-tuple-element.11), channel_id=1, source_target_pairs={{0,0},{1,1},{2,2},{3,3},{4,4},{5,5},{6,6},{7,7},{8,9},{9,8},{10,11... | collective-permute-start | bytes 98312 | tf_op jit(solution)/shard_map/ppermute | solution.py:386
